TPU v7x, 128 devices: a whole 4x4x4 slice. The times are simulated.
128 devices in a mesh: curve: 8 (over x, core), tile: 16 (over z, y).
Axes of the slice: x: 4, y: 4, z: 4, core: 2. Of those that a mesh axis runs over, the one named last changes fastest.
Arguments:
- points: bfloat16 [65536, 512], P(('curve', 'tile')), may hold values from -16 to 16
- neighbours: int32 [27, 65536], P(None, ('curve', 'tile')), may hold values from 448 to 1536, as said below
- conv_weight: bfloat16 [27, 512, 512], replicated, may hold values from -0.078125 to 0.078125
- cpe_gain: float32 [512], replicated, may hold values from 0.1 to 1.9
- w_query: bfloat16 [512, 512], replicated, may hold values from -2 to 2
- w_key: bfloat16 [512, 512], replicated, may hold values from -20 to 20
- w_value: bfloat16 [512, 512], replicated, may hold values from -0.25 to 0.25
- w_out: bfloat16 [512, 512], replicated, may hold values from -0.25 to 0.25
- w_up: bfloat16 [512, 2048], replicated, may hold values from -0.25 to 0.25
- w_down: bfloat16 [2048, 512], replicated, may hold values from -0.125 to 0.125
- w_pool: bfloat16 [512, 512], replicated, may hold values from -0.25 to 0.25
- pool_gain: float32 [512], replicated, may hold values from 0.1 to 1.9
- send_slot: int32 [65536], P(('curve', 'tile')), may hold values from 0 to 1023, as said below
- arrival_from: int32 [131072], P(('curve', 'tile')), may hold values from 0 to 1024, as said below
- pool_pick: int32 [128, 128], P(('curve', 'tile')), may hold values from 0 to 127, each once within a row
- cell_from: int32 [128, 128], P(('curve', 'tile')), may hold values from 0 to 127, each once within a row
Outputs:
- fine_out: bfloat16 [131072, 512], P(('curve', 'tile'))
- pooled: bfloat16 [16384, 512], P(('curve', 'tile'))
Inputs may be any that keep to these rules, and one draw needn't show every extreme that they name: neighbours[13, r] = 512 + r % 512, the point itself; the value 3 * 512 marks a missing neighbour; every other value v satisfies |v - 512 - r % 512| <= 64, so that it lies in 448 .. 1087, and both ends of that range occur in every draw. `send_slot`: the 512 values of one device's points are distinct, so one device sends at most 8 points to one owner; in every draw some owner receives exactly 8 points from every device. `arrival_from`: the 1024 values of one owner name every incoming index that some point has there exactly once, and 1024 in every other slot; in every draw some owner has all its slots filled. `pool_pick`: each owner's row is a permutation of 0 .. 127. `cell_from`: each coarse owner's row is a permutation of 0 .. 127.
All inputs are finite; a program needn't handle non-finite values.
Results may differ from a plain program's by a relative error of at most 0.012.
Values may be sent and summed in bfloat16 or wider, within the bound.
A program may use at most 128 MiB of HBM per device.

v0:
```python
import math

import jax
import jax.numpy as jnp
from jax import lax
from jax.sharding import PartitionSpec as P

HEADS = 32
CAP = 1024
POOL = 8


def with_halo(cells, sides, width):
    for axis, dim in sides:
        count = lax.axis_size(axis)
        ends = count - 1
        head = lax.slice_in_dim(cells, 0, width, axis=dim)
        tail = lax.slice_in_dim(cells, cells.shape[dim] - width, cells.shape[dim], axis=dim)
        cells = jnp.concatenate(
            [
                lax.ppermute(tail, axis, [(i, (i + 1) % count) for i in range(ends)]),
                cells,
                lax.ppermute(head, axis, [((i + 1) % count, i) for i in range(ends)]),
            ],
            axis=dim,
        )
    return cells


def layer_norm(values):
    centre = jnp.mean(values, axis=-1, keepdims=True)
    spread = jnp.mean((values - centre) ** 2, axis=-1, keepdims=True)
    return (values - centre) * lax.rsqrt(spread + 1e-05)


def project(normed, weight_matrix):
    return jnp.dot(normed, weight_matrix, preferred_element_type=jnp.float32).astype(jnp.bfloat16)


def patch_attention(query, keys, values, live):
    slots, width = query.shape
    head_dim = width // HEADS
    per_group = min(HEADS, 4)
    groups = HEADS // per_group
    span = per_group * head_dim
    scale = 1.0 / math.sqrt(head_dim)

    def attend(counter):
        patch = counter // groups
        column = counter % groups * span
        start = patch * CAP
        q_block = lax.dynamic_slice(query, (start, column), (CAP, span)).reshape(
            CAP, per_group, head_dim
        )
        k_block = lax.dynamic_slice(keys, (start, column), (CAP, span)).reshape(
            CAP, per_group, head_dim
        )
        v_block = lax.dynamic_slice(values, (start, column), (CAP, span)).reshape(
            CAP, per_group, head_dim
        )
        scores = (
            jnp.einsum("qhd,khd->hqk", q_block, k_block, preferred_element_type=jnp.float32) * scale
        )
        scores = jnp.where(live[None, None, :], scores, -1e30)
        shifted = jnp.exp(scores - jnp.max(scores, axis=-1, keepdims=True))
        probs = (shifted / jnp.sum(shifted, axis=-1, keepdims=True)).astype(jnp.bfloat16)
        result = jnp.einsum("hqk,khd->qhd", probs, v_block, preferred_element_type=jnp.float32)
        return result.astype(jnp.bfloat16).reshape(CAP, span)

    counters = jnp.arange(slots // CAP * groups, dtype=jnp.int32)
    blocks = lax.map(attend, counters)
    return (
        blocks.reshape(slots // CAP, groups, CAP, span).transpose(0, 2, 1, 3).reshape(slots, width)
    )


def shards(
    points,
    neighbours,
    conv_weight,
    cpe_gain,
    w_query,
    w_key,
    w_value,
    w_out,
    w_up,
    w_down,
    w_pool,
    pool_gain,
    send_slot,
    arrival_from,
    pool_pick,
    cell_from,
):
    local_rows, width = points.shape
    own_slots = arrival_from.shape[0]
    cell_count = pool_pick.shape[1]
    window = with_halo(points, ((("curve", "tile"), 0),), local_rows)
    padded = jnp.concatenate([window, jnp.zeros((1, width), jnp.bfloat16)], axis=0)

    def conv_step(running, carried):
        index_row, weight_slab = carried
        picked = jnp.take(padded, index_row, axis=0)
        return (running + jnp.dot(picked, weight_slab, preferred_element_type=jnp.float32), None)

    conv, _ = lax.scan(
        conv_step, jnp.zeros((local_rows, width), jnp.float32), (neighbours, conv_weight)
    )
    lifted = (points.astype(jnp.float32) + cpe_gain * layer_norm(conv)).astype(jnp.bfloat16)
    stacked = lifted[None]
    layers = stacked.shape[0]
    outgoing = jnp.zeros((layers, own_slots, width), jnp.bfloat16).at[:, send_slot].set(stacked)
    arrived = lax.all_to_all(outgoing, ("curve", "tile"), split_axis=1, concat_axis=1, tiled=True)
    with_blank = jnp.concatenate([arrived, jnp.zeros((layers, 1, width), jnp.bfloat16)], axis=1)
    placed = jnp.take(with_blank, arrival_from, axis=1)
    live = arrival_from < own_slots
    arranged = placed[0]
    normed = layer_norm(arranged.astype(jnp.float32)).astype(jnp.bfloat16)
    query = project(normed, w_query)
    keys = project(normed, w_key)
    values = project(normed, w_value)
    attended = patch_attention(query, keys, values, live)
    mixed = arranged.astype(jnp.float32) + jnp.dot(
        attended, w_out, preferred_element_type=jnp.float32
    )
    second = layer_norm(mixed).astype(jnp.bfloat16)
    inner = jax.nn.gelu(
        jnp.dot(second, w_up, preferred_element_type=jnp.float32), approximate=False
    ).astype(jnp.bfloat16)
    fine = mixed + jnp.dot(inner, w_down, preferred_element_type=jnp.float32)
    fine_out = jnp.where(live[:, None], fine, 0.0).astype(jnp.bfloat16)
    pool_rows = jnp.dot(fine_out, w_pool, preferred_element_type=jnp.float32)
    sums = jnp.sum(pool_rows.reshape(cell_count, POOL, width), axis=1)
    counts = jnp.sum(live.reshape(cell_count, POOL).astype(jnp.float32), axis=1)
    cell_mean = (sums / jnp.maximum(counts, 1.0)[:, None]).astype(jnp.bfloat16)
    sending = jnp.take(cell_mean, pool_pick[0], axis=0)
    landed = lax.all_to_all(sending, ("curve", "tile"), split_axis=0, concat_axis=0, tiled=True)
    gathered = jnp.take(landed, cell_from[0], axis=0)
    pooled = jax.nn.gelu(
        pool_gain * layer_norm(gathered.astype(jnp.float32)), approximate=False
    ).astype(jnp.bfloat16)
    return (fine_out, pooled)


def solution(mesh):
    in_specs = (
        P(("curve", "tile"), None),
        P(None, ("curve", "tile")),
        P(),
        P(),
        P(),
        P(),
        P(),
        P(),
        P(),
        P(),
        P(),
        P(),
        P(("curve", "tile")),
        P(("curve", "tile")),
        P(("curve", "tile"), None),
        P(("curve", "tile"), None),
    )
    out_specs = (P(("curve", "tile"), None), P(("curve", "tile"), None))
    return jax.shard_map(shards, mesh=mesh, in_specs=in_specs, out_specs=out_specs, check_vma=False)
```

profile of v0, /device:TPU:1, one launch (start us, length us, event | category | flops | bytes accessed | tf_op | source)
XLA Modules:
  0.0 512.0 jit_solution(12777522414896411480)
XLA Ops:
  4.8 7.4 %collective-permute-start.1 = (bf16[512,512]{1,0:T(8,128)(2,1)}, bf16[512,512]{1,0:T(8,128)(2,1)}, u32[]{:S(2)}, u32[]{:S(2)}) collective-permute-start(bf16[512,512]{1,0:T(8,128)(2,1)} %param.22), channel_id=1, source_target_pairs={{1,0},{2,1},{3,2},{4,3},{5,4},{6,5},{7,6},{8,7},{9,8},{10,9},{11,1... | collective-permute-start | bytes 1572872 | tf_op jit(solution)/shard_map/ppermute | solution.py:23
  17.5 6.8 %collective-permute-done.1 = bf16[512,512]{1,0:T(8,128)(2,1)} collective-permute-done((bf16[512,512]{1,0:T(8,128)(2,1)}, bf16[512,512]{1,0:T(8,128)(2,1)}, u32[]{:S(2)}, u32[]{:S(2)}) %collective-permute-start.1) | collective-permute-done | bytes 524320 | tf_op jit(solution)/shard_map/ppermute | solution.py:23
  27.2 183.5 %while.24 = (s32[]{:T(128)}, f32[512,512]{1,0:T(8,128)S(1)}, s32[27,512]{1,0:T(8,128)}, bf16[1537,512]{1,0:T(8,128)(2,1)}, bf16[27,512,512]{2,1,0:T(8,128)(2,1)}, /*index=5*/s32[]{:T(128)}, s32[]{:T(128)}) while((s32[]{:T(128)}, f32[512,512]{1,0:T(8,128)S(1)}, s32[27,512]{1,0:T(8,128)}, bf16[1537,512]{1,0:T(8,128)(2,1)}, ...), condition=%wide.region_1.2_spmd.clone, body=%wide.region_0.1_spmd.clone.sunk | while | flops 269227520 | bytes 4212315 | solution.py:106
  27.9 4.3 gather_fusion
  34.7 4.3 gather_fusion
  55.1 4.3 gather_fusion
  68.7 4.3 gather_fusion
  211.1 4.4 scatter_custom_fusion
  220.3 8.0 %reduce = bf16[1024,512]{1,0:T(8,128)(2,1)S(1)} reduce(bf16[1024,1,512]{2,1,0:T(2,128)(2,1)} %bitcast.82, bf16[]{:T(256)} %broadcast.198), dimensions={1}, to_apply=%bitcast.55.reduce_sub_computation | reduce | bytes 2097154
  229.5 10.2 %all-to-all-start = ((bf16[128,2,2048]{2,1,0:T(2,128)(2,1)}), bf16[128,2,2048]{2,1,0:T(2,128)(2,1)S(1)}, u32[]{:S(2)}, u32[]{:S(2)}) async-start(bf16[128,2,2048]{2,1,0:T(2,128)(2,1)} %reshape.212), calls=%async_computation | async-start | bytes 2097152 | tf_op jit(solution)/shard_map/all_to_all | solution.py:113
  242.1 16.3 %all-to-all-done = bf16[128,2,2048]{2,1,0:T(2,128)(2,1)S(1)} async-done(((bf16[128,2,2048]{2,1,0:T(2,128)(2,1)}), bf16[128,2,2048]{2,1,0:T(2,128)(2,1)S(1)}, u32[]{:S(2)}, u32[]{:S(2)}) %all-to-all-start) | async-done | bytes 1048608 | tf_op jit(solution)/shard_map/all_to_all | solution.py:113
  263.8 5.1 gather_fusion.1
  286.2 174.5 %while.23 = (s32[]{:T(128)}, bf16[8,1024,64]{1,2,0:T(8,128)(2,1)}, s32[8]{0:T(128)S(1)}, bf16[1024,512]{0,1:T(8,128)(2,1)}, pred[1024]{0:T(1024)(128)(4,1)S(1)},...) while((s32[]{:T(128)}, bf16[8,1024,64]{1,2,0:T(8,128)(2,1)}, ...), condition=%wide.region_10.11_spmd, body=%wide.region_7.10_spmd.sunk | while | flops 293667840 | bytes 35161900 | solution.py:71
  290.0 9.5 %fusion.131 = (f32[4,1024]{1,0:T(4,128)S(1)}, f32[4,1024,1024]{1,2,0:T(8,128)}) fusion(pred[1024]{0:T(1024)(128)(4,1)S(1)} %get-tuple-element.348, bf16[1024,4,16]{0,2,1:T(8,128)(2,1)S(1)} %bitcast.85, bf16[1024,4,16]{0,2,1:T(8,128)(2,1)S(1)} %bitcast.84), kind=kOutput, calls=%fused_computation.169.clone.1 | convolution fusion | flops 150995968 | bytes 17056768 | tf_op jit(solution)/shard_map/while/body/eval_jaxpr/sub | solution.py:65
  300.4 7.0 %fusion.132 = bf16[4,16,1024]{2,1,0:T(8,128)(2,1)S(1)} fusion(bf16[1024,4,16]{0,2,1:T(8,128)(2,1)S(1)} %bitcast.87, f32[4,1024,1024]{1,2,0:T(8,128)} %get-tuple-element.288, f32[4,1024]{1,0:T(4,128)S(1)} %get-tuple-element.289), kind=kOutput, calls=%fused_computation.15.clone.1 | convolution fusion | flops 142671872 | bytes 17055744 | tf_op jit(solution)/shard_map/while/body/eval_jaxpr/hqk,khd->qhd/dot_general | solution.py:67
  311.8 9.5 %fusion.131 = (f32[4,1024]{1,0:T(4,128)S(1)}, f32[4,1024,1024]{1,2,0:T(8,128)}) fusion(pred[1024]{0:T(1024)(128)(4,1)S(1)} %get-tuple-element.348, bf16[1024,4,16]{0,2,1:T(8,128)(2,1)S(1)} %bitcast.85, bf16[1024,4,16]{0,2,1:T(8,128)(2,1)S(1)} %bitcast.84), kind=kOutput, calls=%fused_computation.169.clone.1 | convolution fusion | flops 150995968 | bytes 17056768 | tf_op jit(solution)/shard_map/while/body/eval_jaxpr/sub | solution.py:65
  322.2 7.0 %fusion.132 = bf16[4,16,1024]{2,1,0:T(8,128)(2,1)S(1)} fusion(bf16[1024,4,16]{0,2,1:T(8,128)(2,1)S(1)} %bitcast.87, f32[4,1024,1024]{1,2,0:T(8,128)} %get-tuple-element.288, f32[4,1024]{1,0:T(4,128)S(1)} %get-tuple-element.289), kind=kOutput, calls=%fused_computation.15.clone.1 | convolution fusion | flops 142671872 | bytes 17055744 | tf_op jit(solution)/shard_map/while/body/eval_jaxpr/hqk,khd->qhd/dot_general | solution.py:67
  333.6 9.5 %fusion.131 = (f32[4,1024]{1,0:T(4,128)S(1)}, f32[4,1024,1024]{1,2,0:T(8,128)}) fusion(pred[1024]{0:T(1024)(128)(4,1)S(1)} %get-tuple-element.348, bf16[1024,4,16]{0,2,1:T(8,128)(2,1)S(1)} %bitcast.85, bf16[1024,4,16]{0,2,1:T(8,128)(2,1)S(1)} %bitcast.84), kind=kOutput, calls=%fused_computation.169.clone.1 | convolution fusion | flops 150995968 | bytes 17056768 | tf_op jit(solution)/shard_map/while/body/eval_jaxpr/sub | solution.py:65
  344.0 7.0 %fusion.132 = bf16[4,16,1024]{2,1,0:T(8,128)(2,1)S(1)} fusion(bf16[1024,4,16]{0,2,1:T(8,128)(2,1)S(1)} %bitcast.87, f32[4,1024,1024]{1,2,0:T(8,128)} %get-tuple-element.288, f32[4,1024]{1,0:T(4,128)S(1)} %get-tuple-element.289), kind=kOutput, calls=%fused_computation.15.clone.1 | convolution fusion | flops 142671872 | bytes 17055744 | tf_op jit(solution)/shard_map/while/body/eval_jaxpr/hqk,khd->qhd/dot_general | solution.py:67
  355.4 9.5 %fusion.131 = (f32[4,1024]{1,0:T(4,128)S(1)}, f32[4,1024,1024]{1,2,0:T(8,128)}) fusion(pred[1024]{0:T(1024)(128)(4,1)S(1)} %get-tuple-element.348, bf16[1024,4,16]{0,2,1:T(8,128)(2,1)S(1)} %bitcast.85, bf16[1024,4,16]{0,2,1:T(8,128)(2,1)S(1)} %bitcast.84), kind=kOutput, calls=%fused_computation.169.clone.1 | convolution fusion | flops 150995968 | bytes 17056768 | tf_op jit(solution)/shard_map/while/body/eval_jaxpr/sub | solution.py:65
  365.8 7.0 %fusion.132 = bf16[4,16,1024]{2,1,0:T(8,128)(2,1)S(1)} fusion(bf16[1024,4,16]{0,2,1:T(8,128)(2,1)S(1)} %bitcast.87, f32[4,1024,1024]{1,2,0:T(8,128)} %get-tuple-element.288, f32[4,1024]{1,0:T(4,128)S(1)} %get-tuple-element.289), kind=kOutput, calls=%fused_computation.15.clone.1 | convolution fusion | flops 142671872 | bytes 17055744 | tf_op jit(solution)/shard_map/while/body/eval_jaxpr/hqk,khd->qhd/dot_general | solution.py:67
  377.2 9.5 %fusion.131 = (f32[4,1024]{1,0:T(4,128)S(1)}, f32[4,1024,1024]{1,2,0:T(8,128)}) fusion(pred[1024]{0:T(1024)(128)(4,1)S(1)} %get-tuple-element.348, bf16[1024,4,16]{0,2,1:T(8,128)(2,1)S(1)} %bitcast.85, bf16[1024,4,16]{0,2,1:T(8,128)(2,1)S(1)} %bitcast.84), kind=kOutput, calls=%fused_computation.169.clone.1 | convolution fusion | flops 150995968 | bytes 17056768 | tf_op jit(solution)/shard_map/while/body/eval_jaxpr/sub | solution.py:65
  387.6 7.0 %fusion.132 = bf16[4,16,1024]{2,1,0:T(8,128)(2,1)S(1)} fusion(bf16[1024,4,16]{0,2,1:T(8,128)(2,1)S(1)} %bitcast.87, f32[4,1024,1024]{1,2,0:T(8,128)} %get-tuple-element.288, f32[4,1024]{1,0:T(4,128)S(1)} %get-tuple-element.289), kind=kOutput, calls=%fused_computation.15.clone.1 | convolution fusion | flops 142671872 | bytes 17055744 | tf_op jit(solution)/shard_map/while/body/eval_jaxpr/hqk,khd->qhd/dot_general | solution.py:67
  399.0 9.5 %fusion.131 = (f32[4,1024]{1,0:T(4,128)S(1)}, f32[4,1024,1024]{1,2,0:T(8,128)}) fusion(pred[1024]{0:T(1024)(128)(4,1)S(1)} %get-tuple-element.348, bf16[1024,4,16]{0,2,1:T(8,128)(2,1)S(1)} %bitcast.85, bf16[1024,4,16]{0,2,1:T(8,128)(2,1)S(1)} %bitcast.84), kind=kOutput, calls=%fused_computation.169.clone.1 | convolution fusion | flops 150995968 | bytes 17056768 | tf_op jit(solution)/shard_map/while/body/eval_jaxpr/sub | solution.py:65
  409.4 7.0 %fusion.132 = bf16[4,16,1024]{2,1,0:T(8,128)(2,1)S(1)} fusion(bf16[1024,4,16]{0,2,1:T(8,128)(2,1)S(1)} %bitcast.87, f32[4,1024,1024]{1,2,0:T(8,128)} %get-tuple-element.288, f32[4,1024]{1,0:T(4,128)S(1)} %get-tuple-element.289), kind=kOutput, calls=%fused_computation.15.clone.1 | convolution fusion | flops 142671872 | bytes 17055744 | tf_op jit(solution)/shard_map/while/body/eval_jaxpr/hqk,khd->qhd/dot_general | solution.py:67
  420.8 9.5 %fusion.131 = (f32[4,1024]{1,0:T(4,128)S(1)}, f32[4,1024,1024]{1,2,0:T(8,128)}) fusion(pred[1024]{0:T(1024)(128)(4,1)S(1)} %get-tuple-element.348, bf16[1024,4,16]{0,2,1:T(8,128)(2,1)S(1)} %bitcast.85, bf16[1024,4,16]{0,2,1:T(8,128)(2,1)S(1)} %bitcast.84), kind=kOutput, calls=%fused_computation.169.clone.1 | convolution fusion | flops 150995968 | bytes 17056768 | tf_op jit(solution)/shard_map/while/body/eval_jaxpr/sub | solution.py:65
  431.2 7.0 %fusion.132 = bf16[4,16,1024]{2,1,0:T(8,128)(2,1)S(1)} fusion(bf16[1024,4,16]{0,2,1:T(8,128)(2,1)S(1)} %bitcast.87, f32[4,1024,1024]{1,2,0:T(8,128)} %get-tuple-element.288, f32[4,1024]{1,0:T(4,128)S(1)} %get-tuple-element.289), kind=kOutput, calls=%fused_computation.15.clone.1 | convolution fusion | flops 142671872 | bytes 17055744 | tf_op jit(solution)/shard_map/while/body/eval_jaxpr/hqk,khd->qhd/dot_general | solution.py:67
  442.7 9.5 %fusion.131 = (f32[4,1024]{1,0:T(4,128)S(1)}, f32[4,1024,1024]{1,2,0:T(8,128)}) fusion(pred[1024]{0:T(1024)(128)(4,1)S(1)} %get-tuple-element.348, bf16[1024,4,16]{0,2,1:T(8,128)(2,1)S(1)} %bitcast.85, bf16[1024,4,16]{0,2,1:T(8,128)(2,1)S(1)} %bitcast.84), kind=kOutput, calls=%fused_computation.169.clone.1 | convolution fusion | flops 150995968 | bytes 17056768 | tf_op jit(solution)/shard_map/while/body/eval_jaxpr/sub | solution.py:65
  453.1 7.0 %fusion.132 = bf16[4,16,1024]{2,1,0:T(8,128)(2,1)S(1)} fusion(bf16[1024,4,16]{0,2,1:T(8,128)(2,1)S(1)} %bitcast.87, f32[4,1024,1024]{1,2,0:T(8,128)} %get-tuple-element.288, f32[4,1024]{1,0:T(4,128)S(1)} %get-tuple-element.289), kind=kOutput, calls=%fused_computation.15.clone.1 | convolution fusion | flops 142671872 | bytes 17055744 | tf_op jit(solution)/shard_map/while/body/eval_jaxpr/hqk,khd->qhd/dot_general | solution.py:67
  464.6 24.8 %select_convert_fusion = bf16[1024,512]{0,1:T(8,128)(2,1)S(1)} fusion(f32[1024,512]{0,1:T(8,128)} %copy-done.1, bf16[2048,512]{1,0:T(8,128)(2,1)S(1)} %copy-done, bf16[512,2048]{1,0:T(8,128)(2,1)} %param.30, f32[1024]{0:T(1024)S(1)} %add_rsqrt_fusion, f32[1024]{0:T(1024)S(1)} %broadcast_multiply_fusion, pred[1024]{0:T(1024)(128)(4,1)S(1)} %get-tuple-element.363), kind=kOutput, calls=%fused_computation.64 | convolution fusion | flops 4434427904 | bytes 7349248 | tf_op jit(solution)/shard_map/dot_general | solution.py:130
  494.0 4.7 all-to-all-start.1
  500.1 9.0 %all-to-all-done.1 = bf16[128,2,256]{2,1,0:T(2,128)(2,1)S(1)} async-done(((bf16[128,2,256]{2,1,0:T(2,128)(2,1)}), bf16[128,2,256]{2,1,0:T(2,128)(2,1)S(1)}, u32[]{:S(2)}, u32[]{:S(2)}) %all-to-all-start.1) | async-done | bytes 131104 | tf_op jit(solution)/shard_map/all_to_all | solution.py:137
  (244 shorter events, 247.9 us)
Async XLA Ops:
  0.6 463.9 %copy-start = (bf16[2048,512]{1,0:T(8,128)(2,1)S(1)}, bf16[2048,512]{1,0:T(8,128)(2,1)}, u32[]{:S(2)}) copy-start(bf16[2048,512]{1,0:T(8,128)(2,1)} %param.31) | copy-start | bytes 6291460
  0.6 16.8 %collective-permute-start = (bf16[512,512]{1,0:T(8,128)(2,1)}, bf16[512,512]{1,0:T(8,128)(2,1)}, u32[]{:S(2)}, u32[]{:S(2)}) collective-permute-start(bf16[512,512]{1,0:T(8,128)(2,1)} %param.22), channel_id=1, source_target_pairs={{0,1},{1,2},{2,3},{3,4},{4,5},{5,6},{6,7},{7,8},{8,9},{9,10},{10,1... | collective-permute-start | bytes 1572872 | tf_op jit(solution)/shard_map/ppermute | solution.py:21
  4.8 19.4 %collective-permute-start.1 = (bf16[512,512]{1,0:T(8,128)(2,1)}, bf16[512,512]{1,0:T(8,128)(2,1)}, u32[]{:S(2)}, u32[]{:S(2)}) collective-permute-start(bf16[512,512]{1,0:T(8,128)(2,1)} %param.22), channel_id=1, source_target_pairs={{1,0},{2,1},{3,2},{4,3},{5,4},{6,5},{7,6},{8,7},{9,8},{10,9},{11,1... | collective-permute-start | bytes 1572872 | tf_op jit(solution)/shard_map/ppermute | solution.py:23
  27.2 184.0 %copy-start.3 = (f32[512]{0:T(512)S(1)}, f32[512]{0:T(512)}, u32[]{:S(2)}) copy-start(f32[512]{0:T(512)} %param.25) | copy-start | bytes 6148
  210.7 29.0 %copy-start.8 = (s32[1,128]{1,0:T(1,128)S(1)}, s32[1,128]{1,0:T(1,128)}, u32[]{:S(2)}) copy-start(s32[1,128]{1,0:T(1,128)} %param.36) | copy-start | bytes 1540
  210.7 30.9 %copy-start.9 = (s32[1,128]{1,0:T(1,128)S(1)}, s32[1,128]{1,0:T(1,128)}, u32[]{:S(2)}) copy-start(s32[1,128]{1,0:T(1,128)} %param.37) | copy-start | bytes 1540
  210.7 31.4 %copy-start.2 = (s32[1024]{0:T(1024)S(1)}, s32[1024]{0:T(1024)}, u32[]{:S(2)}) copy-start(s32[1024]{0:T(1024)} %param.35) | copy-start | bytes 12292
  229.5 28.9 %all-to-all-start = ((bf16[128,2,2048]{2,1,0:T(2,128)(2,1)}), bf16[128,2,2048]{2,1,0:T(2,128)(2,1)S(1)}, u32[]{:S(2)}, u32[]{:S(2)}) async-start(bf16[128,2,2048]{2,1,0:T(2,128)(2,1)} %reshape.212), calls=%async_computation | async-start | bytes 2097152 | tf_op jit(solution)/shard_map/all_to_all | solution.py:113
  462.8 1.4 copy-start.1
  464.5 27.0 %copy-start.6 = (f32[128]{0:T(128)S(1)}, f32[128]{0:T(128)}, u32[]{:S(2)}) copy-start(f32[128]{0:T(128)} %broadcast_maximum_fusion) | copy-start | bytes 1540
  464.5 28.0 %copy-start.5 = (pred[128]{0:T(512)(128)(4,1)S(1)}, pred[128]{0:T(512)(128)(4,1)}, u32[]{:S(2)}) copy-start(pred[128]{0:T(512)(128)(4,1)} %compare_and_fusion.3) | copy-start | bytes 388
  464.5 34.2 %copy-start.10 = (s32[1,128]{1,0:T(1,128)S(1)}, s32[1,128]{1,0:T(1,128)}, u32[]{:S(2)}) copy-start(s32[1,128]{1,0:T(1,128)} %param.37) | copy-start | bytes 1540
  464.5 34.2 %copy-start.7 = (s32[128]{0:T(128)S(1)}, s32[128]{0:T(128)}, u32[]{:S(2)}) copy-start(s32[128]{0:T(128)} %compare_select_fusion.4) | copy-start | bytes 1540
  489.4 21.1 %copy-start.4 = (f32[512]{0:T(512)S(1)}, f32[512]{0:T(512)}, u32[]{:S(2)}) copy-start(f32[512]{0:T(512)} %param.33) | copy-start | bytes 6148
  494.0 15.1 %all-to-all-start.1 = ((bf16[128,2,256]{2,1,0:T(2,128)(2,1)}), bf16[128,2,256]{2,1,0:T(2,128)(2,1)S(1)}, u32[]{:S(2)}, u32[]{:S(2)}) async-start(bf16[128,2,256]{2,1,0:T(2,128)(2,1)} %reshape.214), calls=%async_computation.1 | async-start | bytes 262144 | tf_op jit(solution)/shard_map/all_to_all | solution.py:137
where the time goes:
time: 520 us; the launch traced here: 512 us
  matrix products  217 us (42%)
  local copies, waits for them, and re-layouts  171 us (33%)
  other arithmetic  43.1 us (8%)
  waiting for transfers between devices  35.9 us (7%)
  starting transfers between devices  26.4 us (5%)
  loops' own time  17.4 us (3%)
    gather x27, local copies, waits for them, and re-layouts, conv_step(): picked = jnp.take(padded, index_row, axis=0)  115 us
    sub x8, matrix products, attend(): shifted = jnp.exp(scores - jnp.max(scores, axis=-1, keepdims=True))  75.9 us
    dot_general x8, matrix products, attend(): jnp.einsum('hqk,khd->qhd', probs, v_block, preferred_element_type=jnp.flo...  56 us
    dot_general x27, matrix products, conv_step(): jnp.dot(picked, weight_slab, preferred_element_type=jnp.float32)  47.6 us
    dot_general x1, matrix products, shards(): fine = mixed + jnp.dot(inner, w_down, preferred_element_type=jnp.float32)  24.8 us
    select_n x27, other arithmetic, conv_step(): picked = jnp.take(padded, index_row, axis=0)  19.7 us
    another operation x1, loops' own time, patch_attention(): blocks = lax.map(attend, counters)  16.8 us
    all_to_all x1, waiting for transfers between devices, shards(): lax.all_to_all(outgoing, ('curve', 'tile'), split_axis=1, concat_axis=1,...  16.3 us
  transfers between devices with their start and end apart: 4, of which 4 were waited for; matrix products, arithmetic and copies ran while one was open for 1% of the time, Pallas kernels for 0%

commit v1 on v0

v1 whole, which is shorter than its diff:
```python
import functools
import math

import jax
import jax.numpy as jnp
from jax import lax
from jax.experimental import pallas as pl
from jax.experimental.pallas import tpu as pltpu
from jax.sharding import PartitionSpec as P

F32 = jnp.float32
BF16 = jnp.bfloat16
I32 = jnp.int32

C = 512
HEADS = 32
HEAD = C // HEADS
HID = 2048
KERNEL = 27
OWNERS = 128
OWN = 1024
ROWS = 512
RIM = 64
WIN = 128
BLOCK = 128
GROUP = 3
CHUNKS = KERNEL // GROUP
LANES = 128
GROUPS = C // LANES
PER_GROUP = LANES // HEAD
Q_BLOCK = 512
SCALE = math.log2(math.e) / math.sqrt(HEAD)

VMEM_LIMIT = 60 * 1024 * 1024


def dot(a, b):
    return jnp.dot(a, b, preferred_element_type=F32)


def norm_rows(v):
    centre = jnp.mean(v, axis=-1, keepdims=True)
    shifted = v - centre
    spread = jnp.mean(shifted * shifted, axis=-1, keepdims=True)
    return shifted * lax.rsqrt(spread + 1e-05)


def conv_kernel(window_ref, rel_ref, slot_ref, gain_ref, weight_hbm, out_ref, weight, picked, total, sems):
    copies = [
        pltpu.make_async_copy(
            weight_hbm.at[pl.ds(c * GROUP * C, GROUP * C)],
            weight.at[pl.ds(c * GROUP * C, GROUP * C)],
            sems.at[c],
        )
        for c in range(CHUNKS)
    ]
    for copy in copies:
        copy.start()
    lane = lax.broadcasted_iota(I32, (BLOCK, 2 * BLOCK), 1)
    for c in range(CHUNKS):
        for j in range(GROUP):
            k = c * GROUP + j
            for b in range(ROWS // BLOCK):
                rows = pl.ds(b * BLOCK, BLOCK)
                hot = (rel_ref[rows, k : k + 1] == lane).astype(F32).astype(BF16)
                near = window_ref[pl.ds(b * BLOCK, 2 * BLOCK), :]
                picked[rows, pl.ds(j * C, C)] = dot(hot, near).astype(BF16)
        copies[c].wait()
        part = dot(picked[...], weight[pl.ds(c * GROUP * C, GROUP * C), :])
        if c == 0:
            total[...] = part
        else:
            total[...] += part
    own = window_ref[pl.ds(RIM, ROWS), :].astype(F32)
    lifted = (own + gain_ref[...] * norm_rows(total[...])).astype(BF16)
    slot = lax.broadcasted_iota(I32, (OWN, ROWS), 0)
    hot = (slot == slot_ref[...]).astype(F32).astype(BF16)
    moved = dot(hot, lifted).reshape(OWNERS, 8, C)
    out_ref[...] = jnp.concatenate([moved[:, :, : C // 2], moved[:, :, C // 2 :]], axis=1).astype(BF16)


def conv_call(window, rel, slot, gain, weight):
    vmem = pl.BlockSpec(memory_space=pltpu.VMEM)
    return pl.pallas_call(
        conv_kernel,
        out_shape=jax.ShapeDtypeStruct((OWNERS, 16, C // 2), BF16),
        in_specs=[vmem, vmem, vmem, vmem, pl.BlockSpec(memory_space=pl.ANY)],
        out_specs=vmem,
        scratch_shapes=[
            pltpu.VMEM((KERNEL * C, C), BF16),
            pltpu.VMEM((ROWS, GROUP * C), BF16),
            pltpu.VMEM((ROWS, C), F32),
            pltpu.SemaphoreType.DMA((CHUNKS,)),
        ],
        compiler_params=pltpu.CompilerParams(vmem_limit_bytes=VMEM_LIMIT),
        cost_estimate=pl.CostEstimate(flops=11_000_000_000, bytes_accessed=16_000_000, transcendentals=0),
    )(window, rel, slot, gain, weight)


def owner_kernel(
    arrived_ref, from_row_ref, from_col_ref, pick_ref, wq_hbm, wk_hbm, wv_hbm, wo_hbm, wu_hbm, wd_hbm, wp_hbm,
    fine_ref, sending_ref,
    wq, wk, wv, wo, wu, wd, wp, arranged, query, keys, values, attended, mixed, sems,
):
    pairs = [(wq_hbm, wq), (wk_hbm, wk), (wv_hbm, wv), (wo_hbm, wo), (wu_hbm, wu), (wd_hbm, wd), (wp_hbm, wp)]
    copies = [pltpu.make_async_copy(src, dst, sems.at[i]) for i, (src, dst) in enumerate(pairs)]
    for copy in copies:
        copy.start()
    got = arrived_ref[...].astype(F32)
    got = jnp.concatenate([got[:, :8, :], got[:, 8:, :]], axis=2).astype(BF16).reshape(OWN, C)
    source = lax.broadcasted_iota(I32, (OWN, OWN), 1)
    hot = (from_col_ref[...] == source).astype(F32).astype(BF16)
    placed = dot(hot, got)
    arranged[...] = placed
    normed = norm_rows(placed).astype(BF16)
    live_col = from_col_ref[...] < OWN
    place = lax.broadcasted_iota(I32, (8, OWN), 1)
    first = jnp.min(jnp.where(from_row_ref[...] < OWN, place, OWN), axis=1, keepdims=True)
    stand_in = dot((place == first).astype(F32).astype(BF16), normed)[0:1, :]
    normed_keys = jnp.where(live_col, normed.astype(F32), stand_in).astype(BF16)
    copies[0].wait()
    query[...] = (dot(normed, wq[...]) * SCALE).astype(BF16)
    copies[1].wait()
    keys[...] = dot(normed_keys, wk[...]).astype(BF16)
    copies[2].wait()
    values[...] = dot(normed, wv[...]).astype(BF16)

    lane = lax.broadcasted_iota(I32, (1, LANES), 1)
    live = jnp.broadcast_to(live_col.astype(F32), (OWN, LANES)).astype(BF16)

    @pl.loop(0, GROUPS)
    def _(g):
        columns = pl.ds(pl.multiple_of(g * LANES, LANES), LANES)
        k_group = keys[:, columns]
        v_group = values[:, columns]

        @pl.loop(0, OWN // Q_BLOCK)
        def _(b):
            rows = pl.ds(pl.multiple_of(b * Q_BLOCK, Q_BLOCK), Q_BLOCK)
            q_block = query[rows, columns]
            total = jnp.zeros((Q_BLOCK, 2 * LANES), F32)
            for h in range(PER_GROUP):
                mine = ((lane >= h * HEAD) & (lane < (h + 1) * HEAD)).astype(F32).astype(BF16)
                k_head = k_group * mine
                v_head = jnp.concatenate([v_group * mine, live * mine], axis=1)
                scores = lax.dot_general(q_block, k_head, (((1,), (1,)), ((), ())), preferred_element_type=F32)
                top = jnp.max(scores, axis=1, keepdims=True)
                probs = jnp.exp2((scores - top).astype(BF16))
                total = total + dot(probs, v_head)
            attended[rows, columns] = (total[:, :LANES] / total[:, LANES:]).astype(BF16)

    copies[3].wait()
    mixed[...] = arranged[...] + dot(attended[...], wo[...])
    copies[4].wait()
    copies[5].wait()

    @pl.loop(0, OWN // 256)
    def _(b):
        rows = pl.ds(pl.multiple_of(b * 256, 256), 256)
        mix = mixed[rows, :]
        second = norm_rows(mix).astype(BF16)
        up = dot(second, wu[...])
        inner = (0.5 * up * (1.0 + lax.erf(up * (1.0 / math.sqrt(2.0))))).astype(BF16)
        fine = mix + dot(inner, wd[...])
        fine_ref[rows, :] = jnp.where(from_col_ref[rows, :] < OWN, fine, 0.0).astype(BF16)

    slot = lax.broadcasted_iota(I32, (WIN, OWN), 1) // 8
    cell = lax.broadcasted_iota(I32, (WIN, OWN), 0)
    member = (slot == cell).astype(F32).astype(BF16)
    sums = dot(member, fine_ref[...])
    counts = dot(member, live)[:, 0:1]
    high = sums.astype(BF16)
    low = (sums - high.astype(F32)).astype(BF16)
    copies[6].wait()
    means = ((dot(high, wp[...]) + dot(low, wp[...])) / jnp.maximum(counts, 1.0)).astype(BF16)
    cells = lax.broadcasted_iota(I32, (WIN, WIN), 1)
    sending_ref[...] = dot((pick_ref[...] == cells).astype(F32).astype(BF16), means).astype(BF16)


def owner_call(arrived, from_row, from_col, pick, *weights):
    vmem = pl.BlockSpec(memory_space=pltpu.VMEM)
    hbm = pl.BlockSpec(memory_space=pl.ANY)
    return pl.pallas_call(
        owner_kernel,
        out_shape=(jax.ShapeDtypeStruct((OWN, C), BF16), jax.ShapeDtypeStruct((WIN, C), BF16)),
        in_specs=[vmem] * 4 + [hbm] * 7,
        out_specs=(vmem, vmem),
        scratch_shapes=[
            pltpu.VMEM((C, C), BF16),
            pltpu.VMEM((C, C), BF16),
            pltpu.VMEM((C, C), BF16),
            pltpu.VMEM((C, C), BF16),
            pltpu.VMEM((C, HID), BF16),
            pltpu.VMEM((HID, C), BF16),
            pltpu.VMEM((C, C), BF16),
            pltpu.VMEM((OWN, C), F32),
            pltpu.VMEM((OWN, C), BF16),
            pltpu.VMEM((OWN, C), BF16),
            pltpu.VMEM((OWN, C), BF16),
            pltpu.VMEM((OWN, C), BF16),
            pltpu.VMEM((OWN, C), F32),
            pltpu.SemaphoreType.DMA((7,)),
        ],
        compiler_params=pltpu.CompilerParams(vmem_limit_bytes=VMEM_LIMIT),
        cost_estimate=pl.CostEstimate(flops=40_000_000_000, bytes_accessed=10_000_000, transcendentals=40_000_000),
    )(arrived, from_row, from_col, pick, *weights)


def coarse_kernel(landed_ref, from_ref, gain_ref, out_ref):
    source = lax.broadcasted_iota(I32, (WIN, WIN), 1)
    gathered = dot((from_ref[...] == source).astype(F32).astype(BF16), landed_ref[...])
    value = gain_ref[...] * norm_rows(gathered)
    out_ref[...] = (0.5 * value * (1.0 + lax.erf(value * (1.0 / math.sqrt(2.0))))).astype(BF16)


def coarse_call(landed, cell_from, gain):
    vmem = pl.BlockSpec(memory_space=pltpu.VMEM)
    return pl.pallas_call(
        coarse_kernel,
        out_shape=jax.ShapeDtypeStruct((WIN, C), BF16),
        in_specs=[vmem] * 3,
        out_specs=vmem,
    )(landed, cell_from, gain)


AXES = ("curve", "tile")


def shards(
    points, neighbours, conv_weight, cpe_gain, w_query, w_key, w_value, w_out, w_up, w_down, w_pool, pool_gain,
    send_slot, arrival_from, pool_pick, cell_from,
):
    count = lax.axis_size(AXES)
    before = lax.ppermute(points[ROWS - RIM :], AXES, [(i, i + 1) for i in range(count - 1)])
    after = lax.ppermute(points[:RIM], AXES, [(i + 1, i) for i in range(count - 1)])
    window = jnp.concatenate([before, points, after], axis=0)
    base = ROWS - RIM + BLOCK * (jnp.arange(ROWS, dtype=I32) // BLOCK)
    rel = (neighbours - base[None, :]).T
    outgoing = conv_call(
        window, rel, send_slot[None, :], cpe_gain[None, :], conv_weight.reshape(KERNEL * C, C)
    )
    arrived = lax.all_to_all(outgoing, AXES, split_axis=0, concat_axis=0, tiled=True)
    fine_out, sending = owner_call(
        arrived, arrival_from[None, :], arrival_from[:, None], pool_pick.reshape(WIN, 1),
        w_query, w_key, w_value, w_out, w_up, w_down, w_pool,
    )
    landed = lax.all_to_all(sending, AXES, split_axis=0, concat_axis=0, tiled=True)
    pooled = coarse_call(landed, cell_from.reshape(WIN, 1), pool_gain[None, :])
    return fine_out, pooled


def solution(mesh):
    split = P(AXES)
    rows = P(AXES, None)
    in_specs = (rows, P(None, AXES)) + (P(),) * 10 + (split, split, rows, rows)
    return jax.shard_map(shards, mesh=mesh, in_specs=in_specs, out_specs=(rows, rows), check_vma=False)
```

time: 520 us -> 145 us (0.28); the launches traced: 512 us -> 145 us
  matrix products: 217 us -> 0 us
  local copies, waits for them, and re-layouts: 171 us -> 7.46 us
  Pallas kernels: 0 us -> 81.2 us
  other arithmetic: 43.1 us -> 3.3 us
  loops' own time: 17.4 us -> 0 us
  waiting for transfers between devices: 35.9 us -> 26.6 us
    dot_general x41 -> x0, matrix products: 141 us -> none  [the longest x8 56 us: attend(): jnp.einsum('hqk,khd->qhd', probs, v_block, preferred_element_type=jnp.flo...]
    gather x31 -> x0, local copies, waits for them, and re-layouts: 124 us -> none  [the longest x27 115 us: conv_step(): picked = jnp.take(padded, index_row, axis=0)]
    pallas_call x0 -> x3, Pallas kernels: none -> 81.2 us  [the longest x1 62.5 us: owner_call(): pl.pallas_call(owner_kernel, out_shape=(jax.ShapeDtypeStruct((OWN, C), BF...]
    sub x8 -> x0, matrix products: 75.9 us -> none  [attend(): shifted = jnp.exp(scores - jnp.max(scores, axis=-1, keepdims=True))]
    select_n x30 -> x0, other arithmetic: 20.9 us -> none  [the longest x27 19.7 us: conv_step(): picked = jnp.take(padded, index_row, axis=0)]
    dynamic_slice x24 -> x0, local copies, waits for them, and re-layouts: 20.5 us -> none  [the longest x8 7.93 us: attend(): lax.dynamic_slice(keys, (start, column), (CAP, span))]
    another operation x2 -> x0, loops' own time: 17.4 us -> none  [the longest x1 16.8 us: patch_attention(): blocks = lax.map(attend, counters)]
    ppermute x2, waiting for transfers between devices: 10.6 us -> 0.01 us  [the longest x1 0.01 us: shards(): lax.ppermute(points[ROWS - RIM:], AXES, [(i, i + 1) for i in range(count...]
  transfers between devices with their start and end apart: 4 -> 4, of which waited for: 4 -> 2; matrix products, arithmetic and copies ran while one was open for 1% -> 3% of each run, Pallas kernels for 0% -> 0%
where the time goes in v1:
time: 145 us
  Pallas kernels  81.2 us (56%)
  waiting for transfers between devices  26.6 us (18%)
  starting transfers between devices  25.5 us (18%)
  local copies, waits for them, and re-layouts  7.46 us (5%)
  other arithmetic  3.3 us (2%)
    pallas_call x1, Pallas kernels, owner_call(): pl.pallas_call(owner_kernel, out_shape=(jax.ShapeDtypeStruct((OWN, C), BF...  62.5 us
    all_to_all x1, waiting for transfers between devices, shards(): lax.all_to_all(outgoing, AXES, split_axis=0, concat_axis=0, tiled=True)  17 us
    pallas_call x1, Pallas kernels, conv_call(): pl.pallas_call(conv_kernel, out_shape=jax.ShapeDtypeStruct((OWNERS, 16, C...  16.6 us
    all_to_all x1, waiting for transfers between devices, shards(): lax.all_to_all(sending, AXES, split_axis=0, concat_axis=0, tiled=True)  9.59 us
    all_to_all x1, starting transfers between devices, shards(): lax.all_to_all(outgoing, AXES, split_axis=0, concat_axis=0, tiled=True)  9.35 us
    ppermute x1, starting transfers between devices, shards(): lax.ppermute(points[:RIM], AXES, [(i + 1, i) for i in range(count - 1)])  7.39 us
    all_to_all x1, starting transfers between devices, shards(): lax.all_to_all(sending, AXES, split_axis=0, concat_axis=0, tiled=True)  4.69 us
    ppermute x1, starting transfers between devices, shards(): lax.ppermute(points[ROWS - RIM:], AXES, [(i, i + 1) for i in range(count...  4.03 us
  transfers between devices with their start and end apart: 4, of which 2 were waited for; matrix products, arithmetic and copies ran while one was open for 3% of the time, Pallas kernels for 0%

profile of v1, /device:TPU:1, one launch (start us, length us, event | category | flops | bytes accessed | tf_op | source)
XLA Modules:
  0.0 144.8 jit_solution(4143724868009326258)
XLA Ops:
  0.6 0.0 copy-start.1
  0.6 0.9 fusion.5
  1.6 4.0 %collective-permute-start = (bf16[64,512]{1,0:T(8,128)(2,1)S(1)}, bf16[64,512]{1,0:T(8,128)(2,1)S(1)}, u32[]{:S(2)}, u32[]{:S(2)}) collective-permute-start(bf16[64,512]{1,0:T(8,128)(2,1)S(1)} %get-tuple-element.6), channel_id=1, source_target_pairs={{0,1},{1,2},{2,3},{3,4},{4,5},{5,6},{6,7},{7,8},{8,9},{9,10},{10,1... | collective-permute-start | bytes 196616 | tf_op jit(solution)/shard_map/ppermute | solution.py:234
  5.6 7.4 %collective-permute-start.1 = (bf16[64,512]{1,0:T(8,128)(2,1)S(1)}, bf16[64,512]{1,0:T(8,128)(2,1)S(1)}, u32[]{:S(2)}, u32[]{:S(2)}) collective-permute-start(bf16[64,512]{1,0:T(8,128)(2,1)S(1)} %get-tuple-element.7), channel_id=1, source_target_pairs={{1,0},{2,1},{3,2},{4,3},{5,4},{6,5},{7,6},{8,7},{9,8},{10,9},{11,1... | collective-permute-start | bytes 196616 | tf_op jit(solution)/shard_map/ppermute | solution.py:235
  13.0 1.0 copy.35
  14.0 0.8 subtract_bitcast_fusion.rel_ref
  14.9 0.0 collective-permute-done
  14.9 0.0 collective-permute-done.1
  14.9 0.0 copy-done.1
  14.9 0.9 pad_maximum_fusion.window_ref
  15.8 16.6 %shard_map.167 = bf16[128,16,256]{2,1,0:T(8,128)(2,1)} custom-call(bf16[640,512]{1,0:T(8,128)(2,1)} %pad_maximum_fusion.window_ref, s32[512,27]{1,0:T(8,128)} %subtract_bitcast_fusion.rel_ref, s32[1,512]{1,0:T(1,128)} %bitcast.22, f32[1,512]{1,0:T(1,128)} %bitcast.23, bf16[13824,512]{1,0:T(8,128)(2,1)} %bitcast.21), custom_call_target="tpu_custom_call" | custom-call | flops 11000000512 | bytes 16000000 | tf_op jit(solution)/shard_map/pallas_call | solution.py:84
  32.4 0.0 copy-start.2
  32.4 0.0 copy-start.3
  32.4 9.4 %all-to-all-start = ((bf16[128,16,256]{2,1,0:T(8,128)(2,1)}), bf16[128,16,256]{2,1,0:T(8,128)(2,1)S(1)}, u32[]{:S(2)}, u32[]{:S(2)}) async-start(bf16[128,16,256]{2,1,0:T(8,128)(2,1)} %shard_map.167), calls=%async_computation | async-start | bytes 2097152 | tf_op jit(solution)/shard_map/all_to_all | solution.py:242
  41.8 0.0 copy-done.2
  41.8 1.1 copy.37.from_col_ref
  42.8 0.0 copy-done.3
  42.9 0.7 copy.38.pick_ref
  43.6 17.0 %all-to-all-done.arrived_ref = bf16[128,16,256]{2,1,0:T(8,128)(2,1)S(1)} async-done(((bf16[128,16,256]{2,1,0:T(8,128)(2,1)}), bf16[128,16,256]{2,1,0:T(8,128)(2,1)S(1)}, u32[]{:S(2)}, u32[]{:S(2)}) %all-to-all-start) | async-done | bytes 1048608 | tf_op jit(solution)/shard_map/all_to_all | solution.py:242
  60.6 0.0 copy-start
  60.6 1.0 copy-done
  61.6 62.5 %shard_map.168 = (bf16[1024,512]{1,0:T(8,128)(2,1)}, bf16[128,512]{1,0:T(8,128)(2,1)}) custom-call(bf16[128,16,256]{2,1,0:T(8,128)(2,1)} %copy-done, s32[1,1024]{1,0:T(1,128)} %bitcast.16, s32[1024,1]{1,0:T(8,128)} %copy.37.from_col_ref, s32[128,1]{1,0:T(8,128)} %copy.38.pick_ref, bf16[512,512]{1,0:T(8,128)(2,1)} %wq_hbm.1, bf16[512,512]{1,0:T(8,128)(2,1)} %wk_hbm.1, ...), custom_call_target="tpu_custom_call" | custom-call | flops 40000000000 | bytes 10000000 | tf_op jit(solution)/shard_map/pallas_call | solution.py:183
  124.1 0.5 broadcast.37
  124.6 1.6 %reduce = bf16[128,512]{1,0:T(8,128)(2,1)S(1)} reduce(bf16[128,1,512]{2,0,1:T(8,128)(2,1)} %bitcast.15, bf16[]{:T(256)} %broadcast.37), dimensions={1}, to_apply=%copy.39.reduce_sub_computation | reduce | bytes 262146 | tf_op jit(solution)/shard_map/all_to_all | solution.py:247
  126.2 0.7 reshape.33
  126.9 4.7 %all-to-all-start.1 = ((bf16[128,2,256]{2,1,0:T(2,128)(2,1)}), bf16[128,2,256]{2,1,0:T(2,128)(2,1)S(1)}, u32[]{:S(2)}, u32[]{:S(2)}) async-start(bf16[128,2,256]{2,1,0:T(2,128)(2,1)} %reshape.33), calls=%async_computation.1 | async-start | bytes 262144 | tf_op jit(solution)/shard_map/all_to_all | solution.py:247
  131.6 0.0 copy-done.4
  131.6 0.7 copy.40.from_ref
  132.4 9.6 %all-to-all-done.1 = bf16[128,2,256]{2,1,0:T(2,128)(2,1)S(1)} async-done(((bf16[128,2,256]{2,1,0:T(2,128)(2,1)}), bf16[128,2,256]{2,1,0:T(2,128)(2,1)S(1)}, u32[]{:S(2)}, u32[]{:S(2)}) %all-to-all-start.1) | async-done | bytes 131104 | tf_op jit(solution)/shard_map/all_to_all | solution.py:247
  141.9 0.1 reshape.34
  142.1 0.7 copy.43
  142.7 2.0 %shard_map.169 = bf16[128,512]{1,0:T(8,128)(2,1)} custom-call(bf16[128,512]{1,0:T(8,128)(2,1)} %bitcast.14, s32[128,1]{1,0:T(8,128)} %copy.40.from_ref, f32[1,512]{1,0:T(1,128)} %bitcast.18), custom_call_target="tpu_custom_call" | custom-call | tf_op jit(solution)/shard_map/pallas_call | solution.py:218
  (2 shorter events, 0.0 us)
Async XLA Ops:
  0.6 14.2 %copy-start.1 = (bf16[512,512]{1,0:T(8,128)(2,1)S(1)}, bf16[512,512]{1,0:T(8,128)(2,1)}, u32[]{:S(2)}) copy-start(bf16[512,512]{1,0:T(8,128)(2,1)} %param.16) | copy-start | bytes 1572868
  1.6 13.3 %collective-permute-start = (bf16[64,512]{1,0:T(8,128)(2,1)S(1)}, bf16[64,512]{1,0:T(8,128)(2,1)S(1)}, u32[]{:S(2)}, u32[]{:S(2)}) collective-permute-start(bf16[64,512]{1,0:T(8,128)(2,1)S(1)} %get-tuple-element.6), channel_id=1, source_target_pairs={{0,1},{1,2},{2,3},{3,4},{4,5},{5,6},{6,7},{7,8},{8,9},{9,10},{10,1... | collective-permute-start | bytes 196616 | tf_op jit(solution)/shard_map/ppermute | solution.py:234
  5.6 9.2 %collective-permute-start.1 = (bf16[64,512]{1,0:T(8,128)(2,1)S(1)}, bf16[64,512]{1,0:T(8,128)(2,1)S(1)}, u32[]{:S(2)}, u32[]{:S(2)}) collective-permute-start(bf16[64,512]{1,0:T(8,128)(2,1)S(1)} %get-tuple-element.7), channel_id=1, source_target_pairs={{1,0},{2,1},{3,2},{4,3},{5,4},{6,5},{7,6},{8,7},{9,8},{10,9},{11,1... | collective-permute-start | bytes 196616 | tf_op jit(solution)/shard_map/ppermute | solution.py:235
  32.4 9.4 %copy-start.2 = (s32[1024]{0:T(1024)S(1)}, s32[1024]{0:T(1024)}, u32[]{:S(2)}) copy-start(s32[1024]{0:T(1024)} %param.29) | copy-start | bytes 12292
  32.4 10.5 %copy-start.3 = (s32[1,128]{1,0:T(1,128)S(1)}, s32[1,128]{1,0:T(1,128)}, u32[]{:S(2)}) copy-start(s32[1,128]{1,0:T(1,128)} %param.30) | copy-start | bytes 1540
  32.4 28.2 %all-to-all-start = ((bf16[128,16,256]{2,1,0:T(8,128)(2,1)}), bf16[128,16,256]{2,1,0:T(8,128)(2,1)S(1)}, u32[]{:S(2)}, u32[]{:S(2)}) async-start(bf16[128,16,256]{2,1,0:T(8,128)(2,1)} %shard_map.167), calls=%async_computation | async-start | bytes 2097152 | tf_op jit(solution)/shard_map/all_to_all | solution.py:242
  60.6 1.0 copy-start
  61.6 70.0 %copy-start.4 = (s32[1,128]{1,0:T(1,128)S(1)}, s32[1,128]{1,0:T(1,128)}, u32[]{:S(2)}) copy-start(s32[1,128]{1,0:T(1,128)} %param.31) | copy-start | bytes 1540
  126.9 15.0 %all-to-all-start.1 = ((bf16[128,2,256]{2,1,0:T(2,128)(2,1)}), bf16[128,2,256]{2,1,0:T(2,128)(2,1)S(1)}, u32[]{:S(2)}, u32[]{:S(2)}) async-start(bf16[128,2,256]{2,1,0:T(2,128)(2,1)} %reshape.33), calls=%async_computation.1 | async-start | bytes 262144 | tf_op jit(solution)/shard_map/all_to_all | solution.py:247

commit v2 on v1

v2 whole, which is shorter than its diff:
```python
import math

import jax
import jax.numpy as jnp
from jax import lax
from jax.experimental import pallas as pl
from jax.experimental.pallas import tpu as pltpu
from jax.sharding import PartitionSpec as P

F32 = jnp.float32
BF16 = jnp.bfloat16
I32 = jnp.int32

C = 512
HEADS = 32
HEAD = C // HEADS
HID = 2048
KERNEL = 27
OWNERS = 128
OWN = 1024
ROWS = 512
RIM = 64
WIN = 128
BLOCK = 128
CHUNKS = 9
SPAN = KERNEL * C // CHUNKS
CURVE = 8
TILE = 16
MESH = pl.DeviceIdType.MESH
LANES = 128
GROUPS = C // LANES
PER_GROUP = LANES // HEAD
Q_BLOCK = 512
SCALE = math.log2(math.e) / math.sqrt(HEAD)

VMEM_LIMIT = 60 * 1024 * 1024


def dot(a, b):
    return jnp.dot(a, b, preferred_element_type=F32)


def norm_rows(v):
    centre = jnp.mean(v, axis=-1, keepdims=True)
    shifted = v - centre
    spread = jnp.mean(shifted * shifted, axis=-1, keepdims=True)
    return shifted * lax.rsqrt(spread + 1e-05)


def hot(columns, wanted):
    return (columns == wanted).astype(F32).astype(BF16)


def place_of():
    return lax.axis_index("curve"), lax.axis_index("tile")


def greet(curve, tile):
    barrier = pltpu.get_barrier_semaphore()

    @pl.loop(1, CURVE)
    def _(s):
        pl.semaphore_signal(barrier, inc=1, device_id=(lax.rem(curve + s, CURVE), tile), device_id_type=MESH)

    @pl.loop(1, TILE)
    def _(s):
        pl.semaphore_signal(barrier, inc=1, device_id=(curve, lax.rem(tile + s, TILE)), device_id_type=MESH)

    return barrier


def send(src, dst, sems, i, device):
    pltpu.make_async_remote_copy(
        src_ref=src, dst_ref=dst, send_sem=sems.at[i], recv_sem=sems.at[i + 1], device_id=device, device_id_type=MESH
    ).start()


def drain(ref, sem):
    pltpu.make_async_copy(ref, ref, sem).wait()


class AlongCurve:
    def __init__(self, src, dst, sems, i, curve, tile):
        self.args = src, dst, sems, i, curve, tile

    def start(self):
        src, dst, sems, i, curve, tile = self.args

        @pl.loop(1, CURVE)
        def _(s):
            peer = lax.rem(curve + s, CURVE)
            send(src.at[peer], dst.at[curve], sems, i, (peer, tile))

    def wait_recv(self):
        _, dst, sems, i, _, _ = self.args
        drain(dst.at[pl.ds(0, CURVE - 1)], sems.at[i + 1])

    def wait_send(self):
        src, _, sems, i, _, _ = self.args
        drain(src.at[pl.ds(0, CURVE - 1)], sems.at[i])

    def own(self, sem):
        src, dst, _, _, curve, _ = self.args
        return pltpu.make_async_copy(src.at[curve], dst.at[curve], sem)


class AlongTile:
    def __init__(self, src, dst, sems, i, curve, tile):
        self.args = src, dst, sems, i, curve, tile

    def start(self):
        src, dst, sems, i, curve, tile = self.args

        @pl.loop(1, TILE)
        def _(s):
            peer = lax.rem(tile + s, TILE)
            send(src.at[:, peer], dst.at[:, tile], sems, i, (curve, peer))

    def wait_recv(self):
        _, dst, sems, i, _, _ = self.args
        drain(dst.at[:, pl.ds(0, TILE - 1)], sems.at[i + 1])

    def wait_send(self):
        src, _, sems, i, _, _ = self.args
        drain(src.at[:, pl.ds(0, TILE - 1)], sems.at[i])

    def own(self, sem):
        src, dst, _, _, _, tile = self.args
        return pltpu.make_async_copy(src.at[:, tile], dst.at[:, tile], sem)


def conv_kernel(
    points_ref, near_ref, slot_ref, gain_ref, weight_hbm, left_out, right_out,
    weight, picked, window, total, left_src, right_src, left_mid, right_mid, weight_sems, sems,
):
    curve, tile = place_of()
    me = curve * TILE + tile
    after = lax.rem(me + 1, OWNERS)
    before = lax.rem(me + OWNERS - 1, OWNERS)
    copies = [
        pltpu.make_async_copy(
            weight_hbm.at[pl.ds(c * SPAN, SPAN)], weight.at[pl.ds(c * SPAN, SPAN)], weight_sems.at[c]
        )
        for c in range(CHUNKS)
    ]
    for copy in copies:
        copy.start()
    barrier = greet(curve, tile)
    for peer in (after, before):
        pl.semaphore_signal(
            barrier, inc=1, device_id=(lax.div(peer, TILE), lax.rem(peer, TILE)), device_id_type=MESH
        )
    window[pl.ds(RIM, ROWS), :] = points_ref[...]
    near = near_ref[...] - (ROWS - RIM)
    near = jnp.concatenate([near, jnp.zeros((32 - KERNEL, ROWS), I32)], axis=0).T
    lane = lax.broadcasted_iota(I32, (BLOCK, 2 * BLOCK), 1)

    def pick(b, row):
        local = near[b * BLOCK : (b + 1) * BLOCK] - b * BLOCK
        rows = window[pl.ds(b * BLOCK, 2 * BLOCK), :]
        for k in range(KERNEL):
            picked[pl.ds(row, BLOCK), pl.ds(k * C, C)] = dot(hot(local[:, k : k + 1], lane), rows).astype(BF16)

    def conv(row, count, wait):
        rows = pl.ds(row, count)
        for c in range(CHUNKS):
            if wait:
                copies[c].wait()
            part = dot(picked[rows, pl.ds(c * SPAN, SPAN)], weight[pl.ds(c * SPAN, SPAN), :])
            if c == 0:
                total[rows, :] = part
            else:
                total[rows, :] += part

    pick(1, 1 * BLOCK)
    pick(2, 2 * BLOCK)
    pl.semaphore_wait(barrier, CURVE + TILE)
    low, high = pl.ds(0, RIM), pl.ds(RIM + ROWS, RIM)
    up = pltpu.make_async_remote_copy(
        src_ref=points_ref.at[pl.ds(ROWS - RIM, RIM)], dst_ref=window.at[low], send_sem=sems.at[10],
        recv_sem=sems.at[11], device_id=(lax.div(after, TILE), lax.rem(after, TILE)), device_id_type=MESH,
    )
    down = pltpu.make_async_remote_copy(
        src_ref=points_ref.at[pl.ds(0, RIM)], dst_ref=window.at[high], send_sem=sems.at[12],
        recv_sem=sems.at[13], device_id=(lax.div(before, TILE), lax.rem(before, TILE)), device_id_type=MESH,
    )
    up.start()
    down.start()
    conv(1 * BLOCK, 2 * BLOCK, True)
    up.wait()
    down.wait()

    @pl.when(me == 0)
    def _():
        window[low, :] = jnp.zeros((RIM, C), BF16)

    @pl.when(me == OWNERS - 1)
    def _():
        window[high, :] = jnp.zeros((RIM, C), BF16)

    pick(0, 0)
    pick(3, 3 * BLOCK)
    conv(0, BLOCK, False)
    conv(3 * BLOCK, BLOCK, False)
    lifted = (points_ref[...].astype(F32) + gain_ref[...] * norm_rows(total[...])).astype(BF16)
    slots = hot(lax.broadcasted_iota(I32, (OWN, ROWS), 0), slot_ref[...])

    def outgoing(first):
        moved = dot(slots, lifted[:, first : first + C // 2]).reshape(OWNERS, 8, C // 2)
        blocks = jnp.concatenate([moved[:, :, :LANES], moved[:, :, LANES:]], axis=1).astype(BF16)
        return blocks.reshape(CURVE, TILE, 16, LANES)

    left_one = AlongCurve(left_src, left_mid, sems, 0, curve, tile)
    right_one = AlongTile(right_src, right_mid, sems, 2, curve, tile)
    left_two = AlongTile(left_mid, left_out, sems, 4, curve, tile)
    right_two = AlongCurve(right_mid, right_out, sems, 6, curve, tile)
    left_src[...] = outgoing(0)
    left_one.start()
    left_own = left_one.own(sems.at[8])
    left_own.start()
    right_src[...] = outgoing(C // 2)
    right_one.start()
    right_own = right_one.own(sems.at[9])
    right_own.start()
    left_own.wait()
    left_one.wait_recv()
    left_two.start()
    left_last = left_two.own(sems.at[8])
    left_last.start()
    right_own.wait()
    right_one.wait_recv()
    right_two.start()
    right_last = right_two.own(sems.at[9])
    right_last.start()
    left_last.wait()
    right_last.wait()
    left_two.wait_recv()
    right_two.wait_recv()
    left_one.wait_send()
    right_one.wait_send()
    left_two.wait_send()
    right_two.wait_send()


def conv_call(points, near, slot, gain, weight):
    vmem = pl.BlockSpec(memory_space=pltpu.VMEM)
    half = (CURVE, TILE, 16, LANES)
    return pl.pallas_call(
        conv_kernel,
        out_shape=(jax.ShapeDtypeStruct(half, BF16),) * 2,
        in_specs=[vmem, vmem, vmem, vmem, pl.BlockSpec(memory_space=pl.ANY)],
        out_specs=(vmem, vmem),
        scratch_shapes=[
            pltpu.VMEM((KERNEL * C, C), BF16),
            pltpu.VMEM((ROWS, KERNEL * C), BF16),
            pltpu.VMEM((ROWS + 2 * RIM, C), BF16),
            pltpu.VMEM((ROWS, C), F32),
            pltpu.VMEM(half, BF16),
            pltpu.VMEM(half, BF16),
            pltpu.VMEM(half, BF16),
            pltpu.VMEM(half, BF16),
            pltpu.SemaphoreType.DMA((CHUNKS,)),
            pltpu.SemaphoreType.DMA((14,)),
        ],
        compiler_params=pltpu.CompilerParams(vmem_limit_bytes=VMEM_LIMIT, collective_id=0, has_side_effects=True),
        cost_estimate=pl.CostEstimate(flops=12_000_000_000, bytes_accessed=18_000_000, transcendentals=0),
    )(points, near, slot, gain, weight)


def gelu(v):
    return 0.5 * v * (1.0 + lax.erf(v * (1.0 / math.sqrt(2.0))))


def owner_kernel(
    left_ref, right_ref, from_ref, pick_ref, cell_ref, gain_ref,
    wq_hbm, wk_hbm, wv_hbm, wo_hbm, wu_hbm, wd_hbm, wp_hbm,
    fine_ref, pooled_ref,
    wq, wk, wv, wo, wu, wd, wp, arranged, query, keys, values, attended, mixed,
    cell_src, cell_mid, cell_turn, cell_land, weight_sems, sems,
):
    curve, tile = place_of()
    pairs = [(wq_hbm, wq), (wk_hbm, wk), (wv_hbm, wv), (wo_hbm, wo), (wu_hbm, wu), (wd_hbm, wd), (wp_hbm, wp)]
    copies = [pltpu.make_async_copy(src, dst, weight_sems.at[i]) for i, (src, dst) in enumerate(pairs)]
    for copy in copies:
        copy.start()
    barrier = greet(curve, tile)
    tables = jnp.concatenate([from_ref[...], pick_ref[...], cell_ref[...], jnp.zeros((6, LANES), I32)], axis=0).T
    from_col = jnp.concatenate([tables[:, j : j + 1] for j in range(8)], axis=0)
    pick_col = tables[:, 8:9]
    cell_col = tables[:, 9:10]
    left = left_ref[...].reshape(OWNERS, 16, LANES).astype(F32)
    right = right_ref[...].reshape(OWNERS, 16, LANES).astype(F32)
    got = jnp.concatenate([left[:, :8], left[:, 8:], right[:, :8], right[:, 8:]], axis=2)
    got = got.astype(BF16).reshape(OWN, C)
    placed = dot(hot(from_col, lax.broadcasted_iota(I32, (OWN, OWN), 1)), got)
    arranged[...] = placed
    normed = norm_rows(placed).astype(BF16)
    live_col = from_col < OWN
    place = lax.broadcasted_iota(I32, (8, LANES), 0) * LANES + lax.broadcasted_iota(I32, (8, LANES), 1)
    first = jnp.min(jnp.where(from_ref[...] < OWN, place, OWN), axis=(0, 1), keepdims=True)
    stand_in = dot(hot(lax.broadcasted_iota(I32, (8, OWN), 1), first), normed)[0:1, :]
    normed_keys = jnp.where(live_col, normed.astype(F32), stand_in).astype(BF16)
    copies[0].wait()
    query[...] = (dot(normed, wq[...]) * SCALE).astype(BF16)
    copies[1].wait()
    keys[...] = dot(normed_keys, wk[...]).T.astype(BF16)
    copies[2].wait()
    values[...] = dot(normed, wv[...]).astype(BF16)

    lane = lax.broadcasted_iota(I32, (1, LANES), 1)
    line = lax.broadcasted_iota(I32, (LANES, 1), 0)
    live = jnp.broadcast_to(live_col.astype(F32), (OWN, LANES)).astype(BF16)

    @pl.loop(0, GROUPS)
    def _(g):
        columns = pl.ds(pl.multiple_of(g * LANES, LANES), LANES)
        k_group = keys[columns, :]
        v_group = values[:, columns]

        @pl.loop(0, OWN // Q_BLOCK)
        def _(b):
            rows = pl.ds(pl.multiple_of(b * Q_BLOCK, Q_BLOCK), Q_BLOCK)
            q_block = query[rows, columns]
            all_probs, all_values = [], []
            for h in range(PER_GROUP):
                mine = ((lane >= h * HEAD) & (lane < (h + 1) * HEAD)).astype(F32).astype(BF16)
                mine_lines = ((line >= h * HEAD) & (line < (h + 1) * HEAD)).astype(F32).astype(BF16)
                scores = dot(q_block, k_group * mine_lines)
                top = jnp.max(scores, axis=1, keepdims=True)
                all_probs.append(jnp.exp2(scores - top).astype(BF16))
                all_values.append(jnp.concatenate([v_group * mine, live * mine], axis=1))
            total = dot(jnp.concatenate(all_probs, axis=1), jnp.concatenate(all_values, axis=0))
            attended[rows, columns] = (total[:, :LANES] / total[:, LANES:]).astype(BF16)

    copies[3].wait()
    mixed[...] = arranged[...] + dot(attended[...], wo[...])
    copies[4].wait()
    copies[5].wait()
    for b in range(OWN // 256):
        rows = pl.ds(b * 256, 256)
        mix = mixed[rows, :]
        second = norm_rows(mix).astype(BF16)
        inner = gelu(dot(second, wu[...])).astype(BF16)
        fine = mix + dot(inner, wd[...])
        fine_ref[rows, :] = jnp.where(live_col[b * 256 : (b + 1) * 256], fine, 0.0).astype(BF16)

    slot = lax.broadcasted_iota(I32, (WIN, OWN), 1) // 8
    cell = lax.broadcasted_iota(I32, (WIN, OWN), 0)
    member = hot(slot, cell)
    sums = dot(member, fine_ref[...])
    counts = dot(member, live)[:, 0:1]
    high = sums.astype(BF16)
    low = (sums - high.astype(F32)).astype(BF16)
    copies[6].wait()
    means = ((dot(high, wp[...]) + dot(low, wp[...])) / jnp.maximum(counts, 1.0)).astype(BF16)
    cells = lax.broadcasted_iota(I32, (WIN, WIN), 1)
    cell_src[...] = dot(hot(pick_col, cells), means).astype(BF16).reshape(CURVE, TILE, C)
    one = AlongCurve(cell_src, cell_mid, sems, 0, curve, tile)
    pl.semaphore_wait(barrier, CURVE + TILE - 2)
    one.start()
    own = one.own(sems.at[4])
    own.start()
    own.wait()
    one.wait_recv()
    row = lax.broadcasted_iota(I32, (WIN, 1), 0)
    turned = lax.rem(row, CURVE) * TILE + lax.div(row, CURVE)
    turn = dot(hot(turned, cells), cell_mid[...].reshape(WIN, C)).reshape(TILE, CURVE, C)
    cell_turn[...] = jnp.concatenate([turn[:, :, : C // 2], turn[:, :, C // 2 :]], axis=1).astype(BF16)

    @pl.loop(1, TILE)
    def _(s):
        peer = lax.rem(tile + s, TILE)
        send(cell_turn.at[peer], cell_land.at[tile], sems, 2, (curve, peer))

    own = pltpu.make_async_copy(cell_turn.at[tile], cell_land.at[tile], sems.at[4])
    own.start()
    own.wait()
    drain(cell_land.at[pl.ds(0, TILE - 1)], sems.at[3])
    landed = cell_land[...].astype(F32)
    landed = jnp.concatenate([landed[:, :CURVE], landed[:, CURVE:]], axis=2).astype(BF16).reshape(WIN, C)
    source = lax.rem(cells, CURVE) * TILE + lax.div(cells, CURVE)
    gathered = dot(hot(cell_col, source), landed)
    pooled_ref[...] = gelu(gain_ref[...] * norm_rows(gathered)).astype(BF16)
    one.wait_send()
    drain(cell_turn.at[pl.ds(0, TILE - 1)], sems.at[2])


def owner_call(left, right, from_rows, pick, cell, gain, *weights):
    vmem = pl.BlockSpec(memory_space=pltpu.VMEM)
    hbm = pl.BlockSpec(memory_space=pl.ANY)
    return pl.pallas_call(
        owner_kernel,
        out_shape=(jax.ShapeDtypeStruct((OWN, C), BF16), jax.ShapeDtypeStruct((WIN, C), BF16)),
        in_specs=[vmem] * 6 + [hbm] * 7,
        out_specs=(vmem, vmem),
        scratch_shapes=[
            pltpu.VMEM((C, C), BF16),
            pltpu.VMEM((C, C), BF16),
            pltpu.VMEM((C, C), BF16),
            pltpu.VMEM((C, C), BF16),
            pltpu.VMEM((C, HID), BF16),
            pltpu.VMEM((HID, C), BF16),
            pltpu.VMEM((C, C), BF16),
            pltpu.VMEM((OWN, C), F32),
            pltpu.VMEM((OWN, C), BF16),
            pltpu.VMEM((C, OWN), BF16),
            pltpu.VMEM((OWN, C), BF16),
            pltpu.VMEM((OWN, C), BF16),
            pltpu.VMEM((OWN, C), F32),
            pltpu.VMEM((CURVE, TILE, C), BF16),
            pltpu.VMEM((CURVE, TILE, C), BF16),
            pltpu.VMEM((TILE, 16, C // 2), BF16),
            pltpu.VMEM((TILE, 16, C // 2), BF16),
            pltpu.SemaphoreType.DMA((7,)),
            pltpu.SemaphoreType.DMA((5,)),
        ],
        compiler_params=pltpu.CompilerParams(vmem_limit_bytes=VMEM_LIMIT, collective_id=1, has_side_effects=True),
        cost_estimate=pl.CostEstimate(flops=40_000_000_000, bytes_accessed=10_000_000, transcendentals=40_000_000),
    )(left, right, from_rows, pick, cell, gain, *weights)


AXES = ("curve", "tile")


def shards(
    points, neighbours, conv_weight, cpe_gain, w_query, w_key, w_value, w_out, w_up, w_down, w_pool, pool_gain,
    send_slot, arrival_from, pool_pick, cell_from,
):
    left, right = conv_call(
        points, neighbours, send_slot[None, :], cpe_gain[None, :], conv_weight.reshape(KERNEL * C, C)
    )
    return owner_call(
        left, right, arrival_from.reshape(8, LANES), pool_pick, cell_from, pool_gain[None, :],
        w_query, w_key, w_value, w_out, w_up, w_down, w_pool,
    )


def solution(mesh):
    split = P(AXES)
    rows = P(AXES, None)
    in_specs = (rows, P(None, AXES)) + (P(),) * 10 + (split, split, rows, rows)
    return jax.shard_map(shards, mesh=mesh, in_specs=in_specs, out_specs=(rows, rows), check_vma=False)
```

time: 145 us -> 108 us (0.74)
  waiting for transfers between devices: 26.6 us -> 0 us
  starting transfers between devices: 25.5 us -> 0 us
  Pallas kernels: 81.2 us -> 104 us
  local copies, waits for them, and re-layouts: 7.46 us -> 2.96 us
  other arithmetic: 3.3 us -> 0 us
    all_to_all x2 -> x0, waiting for transfers between devices: 26.6 us -> none  [the longest x1 17 us: shards(): lax.all_to_all(outgoing, AXES, split_axis=0, concat_axis=0, tiled=True)]
    pallas_call x2 -> x1, Pallas kernels: 18.7 us -> 38.3 us  [conv_call(): pl.pallas_call(conv_kernel, out_shape=(jax.ShapeDtypeStruct(half, BF16),)...]
    all_to_all x2 -> x0, starting transfers between devices: 14 us -> none  [the longest x1 9.35 us: shards(): lax.all_to_all(outgoing, AXES, split_axis=0, concat_axis=0, tiled=True)]
    ppermute x2 -> x0, starting transfers between devices: 11.4 us -> none  [the longest x1 7.39 us: shards(): lax.ppermute(points[:RIM], AXES, [(i + 1, i) for i in range(count - 1)])]
    pallas_call x1, Pallas kernels: 62.5 us -> 65.9 us  [owner_call(): pl.pallas_call(owner_kernel, out_shape=(jax.ShapeDtypeStruct((OWN, C), BF...]
    all_to_all x1 -> x0, other arithmetic: 1.57 us -> none  [shards(): lax.all_to_all(sending, AXES, split_axis=0, concat_axis=0, tiled=True)]
    reshape x2 -> x0, local copies, waits for them, and re-layouts: 1.48 us -> none  [the longest x1 0.75 us: shards(): pooled = coarse_call(landed, cell_from.reshape(WIN, 1), pool_gain[None, :])]
    unnamed x14 -> x4, local copies, waits for them, and re-layouts: 3.43 us -> 2.96 us
  transfers between devices with their start and end apart: 4 -> 0, of which waited for: 2 -> 0; matrix products, arithmetic and copies ran while one was open for 3% -> 0% of each run, Pallas kernels for 0% -> 0%
where the time goes in v2:
time: 108 us
  Pallas kernels  104 us (96%)
  local copies, waits for them, and re-layouts  2.96 us (3%)
    pallas_call x1, Pallas kernels, owner_call(): pl.pallas_call(owner_kernel, out_shape=(jax.ShapeDtypeStruct((OWN, C), BF...  65.9 us
    pallas_call x1, Pallas kernels, conv_call(): pl.pallas_call(conv_kernel, out_shape=(jax.ShapeDtypeStruct(half, BF16),)...  38.3 us
    unnamed x4, local copies, waits for them, and re-layouts  2.96 us

profile of v2, /device:TPU:1, one launch (start us, length us, event | category | flops | bytes accessed | tf_op | source)
XLA Modules:
  0.0 107.8 jit_solution(8860673736113692160)
XLA Ops:
  0.6 38.3 %shard_map.167 = (bf16[8,16,16,128]{3,2,1,0:T(8,128)(2,1)}, bf16[8,16,16,128]{3,2,1,0:T(8,128)(2,1)}) custom-call(bf16[512,512]{1,0:T(8,128)(2,1)} %points_ref.1, s32[27,512]{1,0:T(8,128)} %near_ref.1, s32[1,512]{1,0:T(1,128)} %bitcast.7, f32[1,512]{1,0:T(1,128)} %bitcast.8, bf16[13824,512]{1,0:T(8,128)(2,1)} %bitcast.5), custom_call_target="tpu_custom_call" | custom-call | flops 12000000000 | bytes 18000000 | tf_op jit(solution)/shard_map/pallas_call | solution.py:248
  38.9 65.9 %shard_map.168 = (bf16[1024,512]{1,0:T(8,128)(2,1)}, bf16[128,512]{1,0:T(8,128)(2,1)}) custom-call(bf16[8,16,16,128]{3,2,1,0:T(8,128)(2,1)} %get-tuple-element.4.left_ref, bf16[8,16,16,128]{3,2,1,0:T(8,128)(2,1)} %get-tuple-element.5.right_ref, s32[8,128]{1,0:T(8,128)} %bitcast.6, s32[1,128]{1,0:T(1,128)} %pick_ref.1, s32[1,128]{1,0:T(1,128)} %cell_ref.1, ...), custom_call_target="tpu_custom_call" | custom-call | flops 40000000000 | bytes 10000000 | tf_op jit(solution)/shard_map/pallas_call | solution.py:391
  104.8 0.0 copy-start
  104.8 2.3 %copy.20 = bf16[1024,512]{1,0:T(8,128)(2,1)} copy(bf16[1024,512]{1,0:T(8,128)(2,1)} %get-tuple-element.8) | data formatting | bytes 2097152
  107.1 0.0 copy-done
  107.1 0.7 copy.21
Async XLA Ops:
  104.8 2.3 %copy-start = (bf16[128,512]{1,0:T(8,128)(2,1)S(1)}, bf16[128,512]{1,0:T(8,128)(2,1)}, u32[]{:S(2)}) copy-start(bf16[128,512]{1,0:T(8,128)(2,1)} %get-tuple-element.9) | copy-start | bytes 393220

commit v3 on v2

--- a/solution.py
+++ b/solution.py
@@ -10,6 +10,10 @@
 F32 = jnp.float32
 BF16 = jnp.bfloat16
 I32 = jnp.int32
+F8 = jnp.float8_e4m3fn
+SUB = 64
+TOP = 256.0
+TINY = 1e-12
 
 C = 512
 HEADS = 32
@@ -30,7 +34,7 @@
 LANES = 128
 GROUPS = C // LANES
 PER_GROUP = LANES // HEAD
-Q_BLOCK = 512
+Q_BLOCK = 1024
 SCALE = math.log2(math.e) / math.sqrt(HEAD)
 
 VMEM_LIMIT = 60 * 1024 * 1024
@@ -172,8 +176,8 @@
             else:
                 total[rows, :] += part
 
-    pick(1, 1 * BLOCK)
-    pick(2, 2 * BLOCK)
+    pick(1, 0)
+    pick(2, BLOCK)
     pl.semaphore_wait(barrier, CURVE + TILE)
     low, high = pl.ds(0, RIM), pl.ds(RIM + ROWS, RIM)
     up = pltpu.make_async_remote_copy(
@@ -186,7 +190,7 @@
     )
     up.start()
     down.start()
-    conv(1 * BLOCK, 2 * BLOCK, True)
+    conv(0, 2 * BLOCK, True)
     up.wait()
     down.wait()
 
@@ -198,12 +202,13 @@
     def _():
         window[high, :] = jnp.zeros((RIM, C), BF16)
 
-    pick(0, 0)
+    pick(0, 2 * BLOCK)
     pick(3, 3 * BLOCK)
-    conv(0, BLOCK, False)
-    conv(3 * BLOCK, BLOCK, False)
-    lifted = (points_ref[...].astype(F32) + gain_ref[...] * norm_rows(total[...])).astype(BF16)
-    slots = hot(lax.broadcasted_iota(I32, (OWN, ROWS), 0), slot_ref[...])
+    conv(2 * BLOCK, 2 * BLOCK, False)
+    own = jnp.concatenate([points_ref[pl.ds(b * BLOCK, BLOCK), :] for b in (1, 2, 0, 3)], axis=0)
+    lifted = (own.astype(F32) + gain_ref[...] * norm_rows(total[...])).astype(BF16)
+    wanted = jnp.concatenate([slot_ref[:, b * BLOCK : (b + 1) * BLOCK] for b in (1, 2, 0, 3)], axis=1)
+    slots = hot(lax.broadcasted_iota(I32, (OWN, ROWS), 0), wanted)
 
     def outgoing(first):
         moved = dot(slots, lifted[:, first : first + C // 2]).reshape(OWNERS, 8, C // 2)
@@ -272,11 +277,11 @@
 
 
 def owner_kernel(
-    left_ref, right_ref, from_ref, pick_ref, cell_ref, gain_ref,
+    left_ref, right_ref, from_ref, pick_ref,
     wq_hbm, wk_hbm, wv_hbm, wo_hbm, wu_hbm, wd_hbm, wp_hbm,
-    fine_ref, pooled_ref,
+    fine_ref, land_ref,
     wq, wk, wv, wo, wu, wd, wp, arranged, query, keys, values, attended, mixed,
-    cell_src, cell_mid, cell_turn, cell_land, weight_sems, sems,
+    cell_src, cell_mid, cell_turn, weight_sems, sems,
 ):
     curve, tile = place_of()
     pairs = [(wq_hbm, wq), (wk_hbm, wk), (wv_hbm, wv), (wo_hbm, wo), (wu_hbm, wu), (wd_hbm, wd), (wp_hbm, wp)]
@@ -284,10 +289,9 @@
     for copy in copies:
         copy.start()
     barrier = greet(curve, tile)
-    tables = jnp.concatenate([from_ref[...], pick_ref[...], cell_ref[...], jnp.zeros((6, LANES), I32)], axis=0).T
+    tables = jnp.concatenate([from_ref[...], pick_ref[...], jnp.zeros((7, LANES), I32)], axis=0).T
     from_col = jnp.concatenate([tables[:, j : j + 1] for j in range(8)], axis=0)
     pick_col = tables[:, 8:9]
-    cell_col = tables[:, 9:10]
     left = left_ref[...].reshape(OWNERS, 16, LANES).astype(F32)
     right = right_ref[...].reshape(OWNERS, 16, LANES).astype(F32)
     got = jnp.concatenate([left[:, :8], left[:, 8:], right[:, :8], right[:, 8:]], axis=2)
@@ -301,33 +305,55 @@
     stand_in = dot(hot(lax.broadcasted_iota(I32, (8, OWN), 1), first), normed)[0:1, :]
     normed_keys = jnp.where(live_col, normed.astype(F32), stand_in).astype(BF16)
     copies[0].wait()
-    query[...] = (dot(normed, wq[...]) * SCALE).astype(BF16)
+    halves = [wq[:, pl.ds(j * SUB, SUB)] for j in range(C // SUB)]
+    wide = dot(normed, jnp.concatenate([x for half in halves for x in (half, half)], axis=1)) * SCALE
     copies[1].wait()
-    keys[...] = dot(normed_keys, wk[...]).T.astype(BF16)
+    plain = dot(normed_keys, wk[...])
     copies[2].wait()
     values[...] = dot(normed, wv[...]).astype(BF16)
+    most_wide = jnp.maximum(jnp.max(jnp.abs(wide), axis=0, keepdims=True), TINY)
+    most_k = jnp.maximum(jnp.max(jnp.abs(plain), axis=0, keepdims=True), TINY)
+    most_q = jnp.concatenate([most_wide[:, j * LANES : j * LANES + SUB] for j in range(C // SUB)], axis=1)
+    bound = jnp.max(most_q * most_k, axis=1, keepdims=True)
+    grow = TOP * lax.rsqrt(bound)
+    undo = bound * (1.0 / (TOP * TOP))
+    lift = jnp.sqrt(most_k / most_q)
+    lift_wide = jnp.concatenate([lift[:, j // 2 * SUB : j // 2 * SUB + SUB] for j in range(2 * C // SUB)], axis=1)
+    wide = wide * (lift_wide * grow)
+    coarse = wide.astype(F8).astype(F32)
+    first_half = lax.rem(lax.broadcasted_iota(I32, (1, 2 * C), 1), LANES) < SUB
+    query[...] = jnp.where(first_half, wide, wide - coarse).astype(F8)
+    plain = (plain * (grow / lift)).T
+    coarse = plain.astype(F8).astype(F32)
+    keys[0] = coarse.astype(BF16)
+    keys[1] = (plain - coarse).astype(F8).astype(BF16)
 
     lane = lax.broadcasted_iota(I32, (1, LANES), 1)
-    line = lax.broadcasted_iota(I32, (LANES, 1), 0)
+    line = lax.broadcasted_iota(I32, (SUB, 1), 0)
     live = jnp.broadcast_to(live_col.astype(F32), (OWN, LANES)).astype(BF16)
 
     @pl.loop(0, GROUPS)
     def _(g):
         columns = pl.ds(pl.multiple_of(g * LANES, LANES), LANES)
-        k_group = keys[columns, :]
         v_group = values[:, columns]
 
         @pl.loop(0, OWN // Q_BLOCK)
         def _(b):
             rows = pl.ds(pl.multiple_of(b * Q_BLOCK, Q_BLOCK), Q_BLOCK)
-            q_block = query[rows, columns]
             all_probs, all_values = [], []
             for h in range(PER_GROUP):
+                if h % 4 == 0:
+                    part = query[rows, pl.ds(pl.multiple_of(g * 2 * LANES + h // 4 * LANES, LANES), LANES)]
+                    q_block = jnp.concatenate([part, part], axis=1)
+                    lines = pl.ds(pl.multiple_of(g * LANES + h // 4 * SUB, SUB), SUB)
+                    k_high, k_low = keys[0, lines, :], keys[1, lines, :]
+                first = h % 4 * HEAD
                 mine = ((lane >= h * HEAD) & (lane < (h + 1) * HEAD)).astype(F32).astype(BF16)
-                mine_lines = ((line >= h * HEAD) & (line < (h + 1) * HEAD)).astype(F32).astype(BF16)
-                scores = dot(q_block, k_group * mine_lines)
+                mine_lines = ((line >= first) & (line < first + HEAD)).astype(F32).astype(BF16)
+                high, low = (k_high * mine_lines).astype(F8), (k_low * mine_lines).astype(F8)
+                scores = dot(q_block, jnp.concatenate([high, high, low, low], axis=0))
                 top = jnp.max(scores, axis=1, keepdims=True)
-                all_probs.append(jnp.exp2(scores - top).astype(BF16))
+                all_probs.append(jnp.exp2((scores - top) * undo).astype(BF16))
                 all_values.append(jnp.concatenate([v_group * mine, live * mine], axis=1))
             total = dot(jnp.concatenate(all_probs, axis=1), jnp.concatenate(all_values, axis=0))
             attended[rows, columns] = (total[:, :LANES] / total[:, LANES:]).astype(BF16)
@@ -370,28 +396,23 @@
     @pl.loop(1, TILE)
     def _(s):
         peer = lax.rem(tile + s, TILE)
-        send(cell_turn.at[peer], cell_land.at[tile], sems, 2, (curve, peer))
-
-    own = pltpu.make_async_copy(cell_turn.at[tile], cell_land.at[tile], sems.at[4])
+        send(cell_turn.at[peer], land_ref.at[tile], sems, 2, (curve, peer))
+
+    own = pltpu.make_async_copy(cell_turn.at[tile], land_ref.at[tile], sems.at[4])
     own.start()
     own.wait()
-    drain(cell_land.at[pl.ds(0, TILE - 1)], sems.at[3])
-    landed = cell_land[...].astype(F32)
-    landed = jnp.concatenate([landed[:, :CURVE], landed[:, CURVE:]], axis=2).astype(BF16).reshape(WIN, C)
-    source = lax.rem(cells, CURVE) * TILE + lax.div(cells, CURVE)
-    gathered = dot(hot(cell_col, source), landed)
-    pooled_ref[...] = gelu(gain_ref[...] * norm_rows(gathered)).astype(BF16)
+    drain(land_ref.at[pl.ds(0, TILE - 1)], sems.at[3])
     one.wait_send()
     drain(cell_turn.at[pl.ds(0, TILE - 1)], sems.at[2])
 
 
-def owner_call(left, right, from_rows, pick, cell, gain, *weights):
+def owner_call(left, right, from_rows, pick, *weights):
     vmem = pl.BlockSpec(memory_space=pltpu.VMEM)
     hbm = pl.BlockSpec(memory_space=pl.ANY)
     return pl.pallas_call(
         owner_kernel,
-        out_shape=(jax.ShapeDtypeStruct((OWN, C), BF16), jax.ShapeDtypeStruct((WIN, C), BF16)),
-        in_specs=[vmem] * 6 + [hbm] * 7,
+        out_shape=(jax.ShapeDtypeStruct((OWN, C), BF16), jax.ShapeDtypeStruct((TILE, 16, C // 2), BF16)),
+        in_specs=[vmem] * 4 + [hbm] * 7,
         out_specs=(vmem, vmem),
         scratch_shapes=[
             pltpu.VMEM((C, C), BF16),
@@ -402,21 +423,45 @@
             pltpu.VMEM((HID, C), BF16),
             pltpu.VMEM((C, C), BF16),
             pltpu.VMEM((OWN, C), F32),
-            pltpu.VMEM((OWN, C), BF16),
-            pltpu.VMEM((C, OWN), BF16),
+            pltpu.VMEM((OWN, 2 * C), F8),
+            pltpu.VMEM((2, C, OWN), BF16),
             pltpu.VMEM((OWN, C), BF16),
             pltpu.VMEM((OWN, C), BF16),
             pltpu.VMEM((OWN, C), F32),
             pltpu.VMEM((CURVE, TILE, C), BF16),
             pltpu.VMEM((CURVE, TILE, C), BF16),
             pltpu.VMEM((TILE, 16, C // 2), BF16),
-            pltpu.VMEM((TILE, 16, C // 2), BF16),
             pltpu.SemaphoreType.DMA((7,)),
             pltpu.SemaphoreType.DMA((5,)),
         ],
         compiler_params=pltpu.CompilerParams(vmem_limit_bytes=VMEM_LIMIT, collective_id=1, has_side_effects=True),
         cost_estimate=pl.CostEstimate(flops=40_000_000_000, bytes_accessed=10_000_000, transcendentals=40_000_000),
-    )(left, right, from_rows, pick, cell, gain, *weights)
+    )(left, right, from_rows, pick, *weights)
+
+
+def coarse_kernel(fine_ref, land_ref, cell_ref, gain_ref, fine_out, pooled_ref, sem):
+    copy = pltpu.make_async_copy(fine_ref, fine_out, sem)
+    copy.start()
+    cell_col = jnp.concatenate([cell_ref[...], jnp.zeros((7, LANES), I32)], axis=0).T[:, 0:1]
+    cells = lax.broadcasted_iota(I32, (WIN, WIN), 1)
+    landed = land_ref[...].astype(F32)
+    landed = jnp.concatenate([landed[:, :CURVE], landed[:, CURVE:]], axis=2).astype(BF16).reshape(WIN, C)
+    source = lax.rem(cells, CURVE) * TILE + lax.div(cells, CURVE)
+    gathered = dot(hot(cell_col, source), landed)
+    pooled_ref[...] = gelu(gain_ref[...] * norm_rows(gathered)).astype(BF16)
+    copy.wait()
+
+
+def coarse_call(fine, land, cell_from, gain):
+    vmem = pl.BlockSpec(memory_space=pltpu.VMEM)
+    hbm = pl.BlockSpec(memory_space=pl.ANY)
+    return pl.pallas_call(
+        coarse_kernel,
+        out_shape=(jax.ShapeDtypeStruct((OWN, C), BF16), jax.ShapeDtypeStruct((WIN, C), BF16)),
+        in_specs=[hbm, vmem, vmem, vmem],
+        out_specs=(hbm, vmem),
+        scratch_shapes=[pltpu.SemaphoreType.DMA(())],
+    )(fine, land, cell_from, gain)
 
 
 AXES = ("curve", "tile")
@@ -429,10 +474,11 @@
     left, right = conv_call(
         points, neighbours, send_slot[None, :], cpe_gain[None, :], conv_weight.reshape(KERNEL * C, C)
     )
-    return owner_call(
-        left, right, arrival_from.reshape(8, LANES), pool_pick, cell_from, pool_gain[None, :],
+    fine, land = owner_call(
+        left, right, arrival_from.reshape(8, LANES), pool_pick,
         w_query, w_key, w_value, w_out, w_up, w_down, w_pool,
     )
+    return coarse_call(fine, land, cell_from, pool_gain[None, :])
 
 
 def solution(mesh):

time: 108 us -> 136 us (1.26)
  Pallas kernels: 104 us -> 135 us
  local copies, waits for them, and re-layouts: 2.96 us -> 0 us
    pallas_call x0 -> x1, Pallas kernels: none -> 34.5 us  [coarse_call(): pl.pallas_call(coarse_kernel, out_shape=(jax.ShapeDtypeStruct((OWN, C), B...]
    pallas_call x1, Pallas kernels: 65.9 us -> 61.9 us  [owner_call(): pl.pallas_call(owner_kernel, out_shape=(jax.ShapeDtypeStruct((OWN, C), BF...]
    unnamed x4 -> x0, local copies, waits for them, and re-layouts: 2.96 us -> none
where the time goes in v3:
time: 136 us
  Pallas kernels  135 us (99%)
    pallas_call x1, Pallas kernels, owner_call(): pl.pallas_call(owner_kernel, out_shape=(jax.ShapeDtypeStruct((OWN, C), BF...  61.9 us
    pallas_call x1, Pallas kernels, conv_call(): pl.pallas_call(conv_kernel, out_shape=(jax.ShapeDtypeStruct(half, BF16),)...  38.4 us
    pallas_call x1, Pallas kernels, coarse_call(): pl.pallas_call(coarse_kernel, out_shape=(jax.ShapeDtypeStruct((OWN, C), B...  34.5 us

profile of v3, /device:TPU:1, one launch (start us, length us, event | category | flops | bytes accessed | tf_op | source)
XLA Modules:
  0.0 135.5 jit_solution(3832533033430456711)
XLA Ops:
  0.6 38.4 %shard_map.167 = (bf16[8,16,16,128]{3,2,1,0:T(8,128)(2,1)}, bf16[8,16,16,128]{3,2,1,0:T(8,128)(2,1)}) custom-call(bf16[512,512]{1,0:T(8,128)(2,1)} %points_ref.1, s32[27,512]{1,0:T(8,128)} %near_ref.1, s32[1,512]{1,0:T(1,128)} %bitcast.8, f32[1,512]{1,0:T(1,128)} %bitcast.9, bf16[13824,512]{1,0:T(8,128)(2,1)} %bitcast.6), custom_call_target="tpu_custom_call" | custom-call | flops 12000000000 | bytes 18000000 | tf_op jit(solution)/shard_map/pallas_call | solution.py:253
  39.0 61.9 %shard_map.168 = (bf16[1024,512]{1,0:T(8,128)(2,1)}, bf16[16,16,256]{2,1,0:T(8,128)(2,1)}) custom-call(bf16[8,16,16,128]{3,2,1,0:T(8,128)(2,1)} %get-tuple-element.6.left_ref, bf16[8,16,16,128]{3,2,1,0:T(8,128)(2,1)} %get-tuple-element.7.right_ref, s32[8,128]{1,0:T(8,128)} %bitcast.7, s32[1,128]{1,0:T(1,128)} %pick_ref.1, bf16[512,512]{1,0:T(8,128)(2,1)} %wq_hbm.1, ...), custom_call_target="tpu_custom_call" | custom-call | flops 40000000000 | bytes 10000000 | tf_op jit(solution)/shard_map/pallas_call | solution.py:412
  100.9 34.5 %shard_map.169 = (bf16[1024,512]{1,0:T(8,128)(2,1)}, bf16[128,512]{1,0:T(8,128)(2,1)}) custom-call(bf16[1024,512]{1,0:T(8,128)(2,1)} %get-tuple-element.8.fine_ref, bf16[16,16,256]{2,1,0:T(8,128)(2,1)} %get-tuple-element.9.land_ref, s32[1,128]{1,0:T(1,128)} %cell_ref.1, f32[1,512]{1,0:T(1,128)} %bitcast.5), custom_call_target="tpu_custom_call" | custom-call | tf_op jit(solution)/shard_map/pallas_call | solution.py:458

commit v4 on v3

--- a/solution.py
+++ b/solution.py
@@ -458,7 +458,7 @@
     return pl.pallas_call(
         coarse_kernel,
         out_shape=(jax.ShapeDtypeStruct((OWN, C), BF16), jax.ShapeDtypeStruct((WIN, C), BF16)),
-        in_specs=[hbm, vmem, vmem, vmem],
+        in_specs=[vmem] * 4,
         out_specs=(hbm, vmem),
         scratch_shapes=[pltpu.SemaphoreType.DMA(())],
     )(fine, land, cell_from, gain)

time: 136 us -> 104 us (0.76)
  Pallas kernels: 135 us -> 103 us
    pallas_call x1, Pallas kernels: 34.5 us -> 2.94 us  [coarse_call(): pl.pallas_call(coarse_kernel, out_shape=(jax.ShapeDtypeStruct((OWN, C), B...]
where the time goes in v4:
time: 104 us
  Pallas kernels  103 us (99%)
    pallas_call x1, Pallas kernels, owner_call(): pl.pallas_call(owner_kernel, out_shape=(jax.ShapeDtypeStruct((OWN, C), BF...  61.9 us
    pallas_call x1, Pallas kernels, conv_call(): pl.pallas_call(conv_kernel, out_shape=(jax.ShapeDtypeStruct(half, BF16),)...  38.4 us
    pallas_call x1, Pallas kernels, coarse_call(): pl.pallas_call(coarse_kernel, out_shape=(jax.ShapeDtypeStruct((OWN, C), B...  2.94 us

profile of v4, /device:TPU:1, one launch (start us, length us, event | category | flops | bytes accessed | tf_op | source)
XLA Modules:
  0.0 104.0 jit_solution(9941808883405614745)
XLA Ops:
  0.6 38.4 %shard_map.167 = (bf16[8,16,16,128]{3,2,1,0:T(8,128)(2,1)}, bf16[8,16,16,128]{3,2,1,0:T(8,128)(2,1)}) custom-call(bf16[512,512]{1,0:T(8,128)(2,1)} %points_ref.1, s32[27,512]{1,0:T(8,128)} %near_ref.1, s32[1,512]{1,0:T(1,128)} %bitcast.8, f32[1,512]{1,0:T(1,128)} %bitcast.9, bf16[13824,512]{1,0:T(8,128)(2,1)} %bitcast.6), custom_call_target="tpu_custom_call" | custom-call | flops 12000000000 | bytes 18000000 | tf_op jit(solution)/shard_map/pallas_call | solution.py:253
  39.0 61.9 %shard_map.168 = (bf16[1024,512]{1,0:T(8,128)(2,1)}, bf16[16,16,256]{2,1,0:T(8,128)(2,1)}) custom-call(bf16[8,16,16,128]{3,2,1,0:T(8,128)(2,1)} %get-tuple-element.6.left_ref, bf16[8,16,16,128]{3,2,1,0:T(8,128)(2,1)} %get-tuple-element.7.right_ref, s32[8,128]{1,0:T(8,128)} %bitcast.7, s32[1,128]{1,0:T(1,128)} %pick_ref.1, bf16[512,512]{1,0:T(8,128)(2,1)} %wq_hbm.1, ...), custom_call_target="tpu_custom_call" | custom-call | flops 40000000000 | bytes 10000000 | tf_op jit(solution)/shard_map/pallas_call | solution.py:412
  100.9 2.9 %shard_map.169 = (bf16[1024,512]{1,0:T(8,128)(2,1)}, bf16[128,512]{1,0:T(8,128)(2,1)}) custom-call(bf16[1024,512]{1,0:T(8,128)(2,1)} %get-tuple-element.8.fine_ref, bf16[16,16,256]{2,1,0:T(8,128)(2,1)} %get-tuple-element.9.land_ref, s32[1,128]{1,0:T(1,128)} %cell_ref.1, f32[1,512]{1,0:T(1,128)} %bitcast.5), custom_call_target="tpu_custom_call" | custom-call | tf_op jit(solution)/shard_map/pallas_call | solution.py:458

commit v5 on v4

--- a/solution.py
+++ b/solution.py
@@ -34,10 +34,10 @@
 LANES = 128
 GROUPS = C // LANES
 PER_GROUP = LANES // HEAD
-Q_BLOCK = 1024
+Q_BLOCK = 512
 SCALE = math.log2(math.e) / math.sqrt(HEAD)
 
-VMEM_LIMIT = 60 * 1024 * 1024
+VMEM_LIMIT = 62 * 1024 * 1024
 
 
 def dot(a, b):
@@ -133,9 +133,16 @@
         return pltpu.make_async_copy(src.at[:, tile], dst.at[:, tile], sem)
 
 
-def conv_kernel(
-    points_ref, near_ref, slot_ref, gain_ref, weight_hbm, left_out, right_out,
-    weight, picked, window, total, left_src, right_src, left_mid, right_mid, weight_sems, sems,
+def gelu(v):
+    return 0.5 * v * (1.0 + lax.erf(v * (1.0 / math.sqrt(2.0))))
+
+
+def block_kernel(
+    points_ref, near_ref, slot_ref, gain_ref, from_ref, pick_ref,
+    weight_hbm, wq_hbm, wk_hbm, wv_hbm, wo_hbm, wu_hbm, wd_hbm, wp_hbm,
+    fine_ref, land_ref,
+    weight, picked, window, total, left_src, right_src, left_mid, right_mid, left_out, right_out,
+    arranged, query, keys, mixed, cell_src, cell_mid, cell_turn, weight_sems, late_sems, sems, cell_sems,
 ):
     curve, tile = place_of()
     me = curve * TILE + tile
@@ -165,12 +172,12 @@
         for k in range(KERNEL):
             picked[pl.ds(row, BLOCK), pl.ds(k * C, C)] = dot(hot(local[:, k : k + 1], lane), rows).astype(BF16)
 
-    def conv(row, count, wait):
-        rows = pl.ds(row, count)
+    def conv(row, wait):
+        rows = pl.ds(row, 2 * BLOCK)
         for c in range(CHUNKS):
             if wait:
                 copies[c].wait()
-            part = dot(picked[rows, pl.ds(c * SPAN, SPAN)], weight[pl.ds(c * SPAN, SPAN), :])
+            part = dot(picked[:, pl.ds(c * SPAN, SPAN)], weight[pl.ds(c * SPAN, SPAN), :])
             if c == 0:
                 total[rows, :] = part
             else:
@@ -190,7 +197,7 @@
     )
     up.start()
     down.start()
-    conv(0, 2 * BLOCK, True)
+    conv(0, True)
     up.wait()
     down.wait()
 
@@ -202,9 +209,9 @@
     def _():
         window[high, :] = jnp.zeros((RIM, C), BF16)
 
-    pick(0, 2 * BLOCK)
-    pick(3, 3 * BLOCK)
-    conv(2 * BLOCK, 2 * BLOCK, False)
+    pick(0, 0)
+    pick(3, BLOCK)
+    conv(2 * BLOCK, False)
     own = jnp.concatenate([points_ref[pl.ds(b * BLOCK, BLOCK), :] for b in (1, 2, 0, 3)], axis=0)
     lifted = (own.astype(F32) + gain_ref[...] * norm_rows(total[...])).astype(BF16)
     wanted = jnp.concatenate([slot_ref[:, b * BLOCK : (b + 1) * BLOCK] for b in (1, 2, 0, 3)], axis=1)
@@ -227,6 +234,25 @@
     right_one.start()
     right_own = right_one.own(sems.at[9])
     right_own.start()
+
+    def room(first, count):
+        return weight.at[pl.ds(first, count)]
+
+    wq, wk, wv, wo, wp = (room(i * C, C) for i in range(5))
+    wd = room(5 * C, HID)
+    ups = [room(9 * C + j * C, C) for j in range(HID // C)]
+    values, attended = room(13 * C, OWN), room(15 * C, OWN)
+    pairs = [(wq_hbm, wq), (wk_hbm, wk), (wv_hbm, wv), (wo_hbm, wo), (wp_hbm, wp), (wd_hbm, wd)]
+    pairs += [(wu_hbm.at[:, pl.ds(j * C, C)], ups[j]) for j in range(HID // C)]
+    copies = [pltpu.make_async_copy(src, dst, late_sems.at[i]) for i, (src, dst) in enumerate(pairs)]
+    for copy in copies:
+        copy.start()
+    tables = jnp.concatenate([from_ref[...], pick_ref[...], jnp.zeros((7, LANES), I32)], axis=0).T
+    from_col = jnp.concatenate([tables[:, j : j + 1] for j in range(8)], axis=0)
+    pick_col = tables[:, 8:9]
+    source = lax.broadcasted_iota(I32, (2 * BLOCK, OWN), 1)
+    for j in range(4):
+        picked[:, pl.ds(j * OWN, OWN)] = hot(from_col[j * 2 * BLOCK : (j + 1) * 2 * BLOCK], source)
     left_own.wait()
     left_one.wait_recv()
     left_two.start()
@@ -245,58 +271,11 @@
     right_one.wait_send()
     left_two.wait_send()
     right_two.wait_send()
-
-
-def conv_call(points, near, slot, gain, weight):
-    vmem = pl.BlockSpec(memory_space=pltpu.VMEM)
-    half = (CURVE, TILE, 16, LANES)
-    return pl.pallas_call(
-        conv_kernel,
-        out_shape=(jax.ShapeDtypeStruct(half, BF16),) * 2,
-        in_specs=[vmem, vmem, vmem, vmem, pl.BlockSpec(memory_space=pl.ANY)],
-        out_specs=(vmem, vmem),
-        scratch_shapes=[
-            pltpu.VMEM((KERNEL * C, C), BF16),
-            pltpu.VMEM((ROWS, KERNEL * C), BF16),
-            pltpu.VMEM((ROWS + 2 * RIM, C), BF16),
-            pltpu.VMEM((ROWS, C), F32),
-            pltpu.VMEM(half, BF16),
-            pltpu.VMEM(half, BF16),
-            pltpu.VMEM(half, BF16),
-            pltpu.VMEM(half, BF16),
-            pltpu.SemaphoreType.DMA((CHUNKS,)),
-            pltpu.SemaphoreType.DMA((14,)),
-        ],
-        compiler_params=pltpu.CompilerParams(vmem_limit_bytes=VMEM_LIMIT, collective_id=0, has_side_effects=True),
-        cost_estimate=pl.CostEstimate(flops=12_000_000_000, bytes_accessed=18_000_000, transcendentals=0),
-    )(points, near, slot, gain, weight)
-
-
-def gelu(v):
-    return 0.5 * v * (1.0 + lax.erf(v * (1.0 / math.sqrt(2.0))))
-
-
-def owner_kernel(
-    left_ref, right_ref, from_ref, pick_ref,
-    wq_hbm, wk_hbm, wv_hbm, wo_hbm, wu_hbm, wd_hbm, wp_hbm,
-    fine_ref, land_ref,
-    wq, wk, wv, wo, wu, wd, wp, arranged, query, keys, values, attended, mixed,
-    cell_src, cell_mid, cell_turn, weight_sems, sems,
-):
-    curve, tile = place_of()
-    pairs = [(wq_hbm, wq), (wk_hbm, wk), (wv_hbm, wv), (wo_hbm, wo), (wu_hbm, wu), (wd_hbm, wd), (wp_hbm, wp)]
-    copies = [pltpu.make_async_copy(src, dst, weight_sems.at[i]) for i, (src, dst) in enumerate(pairs)]
-    for copy in copies:
-        copy.start()
-    barrier = greet(curve, tile)
-    tables = jnp.concatenate([from_ref[...], pick_ref[...], jnp.zeros((7, LANES), I32)], axis=0).T
-    from_col = jnp.concatenate([tables[:, j : j + 1] for j in range(8)], axis=0)
-    pick_col = tables[:, 8:9]
-    left = left_ref[...].reshape(OWNERS, 16, LANES).astype(F32)
-    right = right_ref[...].reshape(OWNERS, 16, LANES).astype(F32)
+    left = left_out[...].reshape(OWNERS, 16, LANES).astype(F32)
+    right = right_out[...].reshape(OWNERS, 16, LANES).astype(F32)
     got = jnp.concatenate([left[:, :8], left[:, 8:], right[:, :8], right[:, 8:]], axis=2)
     got = got.astype(BF16).reshape(OWN, C)
-    placed = dot(hot(from_col, lax.broadcasted_iota(I32, (OWN, OWN), 1)), got)
+    placed = jnp.concatenate([dot(picked[:, pl.ds(j * OWN, OWN)], got) for j in range(4)], axis=0)
     arranged[...] = placed
     normed = norm_rows(placed).astype(BF16)
     live_col = from_col < OWN
@@ -360,13 +339,13 @@
 
     copies[3].wait()
     mixed[...] = arranged[...] + dot(attended[...], wo[...])
-    copies[4].wait()
-    copies[5].wait()
+    for copy in copies[5:]:
+        copy.wait()
     for b in range(OWN // 256):
         rows = pl.ds(b * 256, 256)
         mix = mixed[rows, :]
         second = norm_rows(mix).astype(BF16)
-        inner = gelu(dot(second, wu[...])).astype(BF16)
+        inner = jnp.concatenate([gelu(dot(second, up[...])).astype(BF16) for up in ups], axis=1)
         fine = mix + dot(inner, wd[...])
         fine_ref[rows, :] = jnp.where(live_col[b * 256 : (b + 1) * 256], fine, 0.0).astype(BF16)
 
@@ -377,14 +356,13 @@
     counts = dot(member, live)[:, 0:1]
     high = sums.astype(BF16)
     low = (sums - high.astype(F32)).astype(BF16)
-    copies[6].wait()
+    copies[4].wait()
     means = ((dot(high, wp[...]) + dot(low, wp[...])) / jnp.maximum(counts, 1.0)).astype(BF16)
     cells = lax.broadcasted_iota(I32, (WIN, WIN), 1)
     cell_src[...] = dot(hot(pick_col, cells), means).astype(BF16).reshape(CURVE, TILE, C)
-    one = AlongCurve(cell_src, cell_mid, sems, 0, curve, tile)
-    pl.semaphore_wait(barrier, CURVE + TILE - 2)
+    one = AlongCurve(cell_src, cell_mid, cell_sems, 0, curve, tile)
     one.start()
-    own = one.own(sems.at[4])
+    own = one.own(cell_sems.at[4])
     own.start()
     own.wait()
     one.wait_recv()
@@ -396,47 +374,48 @@
     @pl.loop(1, TILE)
     def _(s):
         peer = lax.rem(tile + s, TILE)
-        send(cell_turn.at[peer], land_ref.at[tile], sems, 2, (curve, peer))
-
-    own = pltpu.make_async_copy(cell_turn.at[tile], land_ref.at[tile], sems.at[4])
+        send(cell_turn.at[peer], land_ref.at[tile], cell_sems, 2, (curve, peer))
+
+    own = pltpu.make_async_copy(cell_turn.at[tile], land_ref.at[tile], cell_sems.at[4])
     own.start()
     own.wait()
-    drain(land_ref.at[pl.ds(0, TILE - 1)], sems.at[3])
+    drain(land_ref.at[pl.ds(0, TILE - 1)], cell_sems.at[3])
     one.wait_send()
-    drain(cell_turn.at[pl.ds(0, TILE - 1)], sems.at[2])
-
-
-def owner_call(left, right, from_rows, pick, *weights):
+    drain(cell_turn.at[pl.ds(0, TILE - 1)], cell_sems.at[2])
+
+
+def block_call(*args):
     vmem = pl.BlockSpec(memory_space=pltpu.VMEM)
     hbm = pl.BlockSpec(memory_space=pl.ANY)
+    half = (CURVE, TILE, 16, LANES)
     return pl.pallas_call(
-        owner_kernel,
+        block_kernel,
         out_shape=(jax.ShapeDtypeStruct((OWN, C), BF16), jax.ShapeDtypeStruct((TILE, 16, C // 2), BF16)),
-        in_specs=[vmem] * 4 + [hbm] * 7,
+        in_specs=[vmem] * 6 + [hbm] * 8,
         out_specs=(vmem, vmem),
         scratch_shapes=[
-            pltpu.VMEM((C, C), BF16),
-            pltpu.VMEM((C, C), BF16),
-            pltpu.VMEM((C, C), BF16),
-            pltpu.VMEM((C, C), BF16),
-            pltpu.VMEM((C, HID), BF16),
-            pltpu.VMEM((HID, C), BF16),
-            pltpu.VMEM((C, C), BF16),
+            pltpu.VMEM((KERNEL * C, C), BF16),
+            pltpu.VMEM((2 * BLOCK, KERNEL * C), BF16),
+            pltpu.VMEM((ROWS + 2 * RIM, C), BF16),
+            pltpu.VMEM((ROWS, C), F32),
+        ]
+        + [pltpu.VMEM(half, BF16)] * 6
+        + [
             pltpu.VMEM((OWN, C), F32),
             pltpu.VMEM((OWN, 2 * C), F8),
             pltpu.VMEM((2, C, OWN), BF16),
-            pltpu.VMEM((OWN, C), BF16),
-            pltpu.VMEM((OWN, C), BF16),
             pltpu.VMEM((OWN, C), F32),
             pltpu.VMEM((CURVE, TILE, C), BF16),
             pltpu.VMEM((CURVE, TILE, C), BF16),
             pltpu.VMEM((TILE, 16, C // 2), BF16),
-            pltpu.SemaphoreType.DMA((7,)),
+            pltpu.SemaphoreType.DMA((CHUNKS,)),
+            pltpu.SemaphoreType.DMA((10,)),
+            pltpu.SemaphoreType.DMA((14,)),
             pltpu.SemaphoreType.DMA((5,)),
         ],
-        compiler_params=pltpu.CompilerParams(vmem_limit_bytes=VMEM_LIMIT, collective_id=1, has_side_effects=True),
-        cost_estimate=pl.CostEstimate(flops=40_000_000_000, bytes_accessed=10_000_000, transcendentals=40_000_000),
-    )(left, right, from_rows, pick, *weights)
+        compiler_params=pltpu.CompilerParams(vmem_limit_bytes=VMEM_LIMIT, collective_id=0, has_side_effects=True),
+        cost_estimate=pl.CostEstimate(flops=50_000_000_000, bytes_accessed=25_000_000, transcendentals=40_000_000),
+    )(*args)
 
 
 def coarse_kernel(fine_ref, land_ref, cell_ref, gain_ref, fine_out, pooled_ref, sem):
@@ -471,12 +450,9 @@
     points, neighbours, conv_weight, cpe_gain, w_query, w_key, w_value, w_out, w_up, w_down, w_pool, pool_gain,
     send_slot, arrival_from, pool_pick, cell_from,
 ):
-    left, right = conv_call(
-        points, neighbours, send_slot[None, :], cpe_gain[None, :], conv_weight.reshape(KERNEL * C, C)
-    )
-    fine, land = owner_call(
-        left, right, arrival_from.reshape(8, LANES), pool_pick,
-        w_query, w_key, w_value, w_out, w_up, w_down, w_pool,
+    fine, land = block_call(
+        points, neighbours, send_slot[None, :], cpe_gain[None, :], arrival_from.reshape(8, LANES), pool_pick,
+        conv_weight.reshape(KERNEL * C, C), w_query, w_key, w_value, w_out, w_up, w_down, w_pool,
     )
     return coarse_call(fine, land, cell_from, pool_gain[None, :])
 

time: 104 us -> 102 us (0.981)
  Pallas kernels: 103 us -> 101 us
    pallas_call x2 -> x1, Pallas kernels: 100 us -> 98.2 us  [block_call(): pl.pallas_call(block_kernel, out_shape=(jax.ShapeDtypeStruct((OWN, C), BF...]
where the time goes in v5:
time: 102 us
  Pallas kernels  101 us (99%)
    pallas_call x1, Pallas kernels, block_call(): pl.pallas_call(block_kernel, out_shape=(jax.ShapeDtypeStruct((OWN, C), BF...  98.2 us
    pallas_call x1, Pallas kernels, coarse_call(): pl.pallas_call(coarse_kernel, out_shape=(jax.ShapeDtypeStruct((OWN, C), B...  2.94 us

profile of v5, /device:TPU:1, one launch (start us, length us, event | category | flops | bytes accessed | tf_op | source)
XLA Modules:
  0.0 101.9 jit_solution(1929807422009940876)
XLA Ops:
  0.6 98.2 %shard_map.167 = (bf16[1024,512]{1,0:T(8,128)(2,1)}, bf16[16,16,256]{2,1,0:T(8,128)(2,1)}) custom-call(bf16[512,512]{1,0:T(8,128)(2,1)} %points_ref.1, s32[27,512]{1,0:T(8,128)} %near_ref.1, s32[1,512]{1,0:T(1,128)} %bitcast.8, f32[1,512]{1,0:T(1,128)} %bitcast.9, s32[8,128]{1,0:T(8,128)} %bitcast.7, s32[1,128]{1,0:T(1,128)} %pick_ref.1, ...), custom_call_target="tpu_custom_call" | custom-call | flops 49999998976 | bytes 25000000 | tf_op jit(solution)/shard_map/pallas_call | solution.py:391
  98.8 2.9 %shard_map.168 = (bf16[1024,512]{1,0:T(8,128)(2,1)}, bf16[128,512]{1,0:T(8,128)(2,1)}) custom-call(bf16[1024,512]{1,0:T(8,128)(2,1)} %get-tuple-element.4.fine_ref, bf16[16,16,256]{2,1,0:T(8,128)(2,1)} %get-tuple-element.5.land_ref, s32[1,128]{1,0:T(1,128)} %cell_ref.1, f32[1,512]{1,0:T(1,128)} %bitcast.5), custom_call_target="tpu_custom_call" | custom-call | tf_op jit(solution)/shard_map/pallas_call | solution.py:437

commit v6 on v5

--- a/solution.py
+++ b/solution.py
@@ -35,6 +35,7 @@
 GROUPS = C // LANES
 PER_GROUP = LANES // HEAD
 Q_BLOCK = 512
+PIECES = 4
 SCALE = math.log2(math.e) / math.sqrt(HEAD)
 
 VMEM_LIMIT = 62 * 1024 * 1024
@@ -62,12 +63,9 @@
 def greet(curve, tile):
     barrier = pltpu.get_barrier_semaphore()
 
-    @pl.loop(1, CURVE)
-    def _(s):
+    for s in range(1, CURVE):
         pl.semaphore_signal(barrier, inc=1, device_id=(lax.rem(curve + s, CURVE), tile), device_id_type=MESH)
-
-    @pl.loop(1, TILE)
-    def _(s):
+    for s in range(1, TILE):
         pl.semaphore_signal(barrier, inc=1, device_id=(curve, lax.rem(tile + s, TILE)), device_id_type=MESH)
 
     return barrier
@@ -141,7 +139,7 @@
     points_ref, near_ref, slot_ref, gain_ref, from_ref, pick_ref,
     weight_hbm, wq_hbm, wk_hbm, wv_hbm, wo_hbm, wu_hbm, wd_hbm, wp_hbm,
     fine_ref, land_ref,
-    weight, picked, window, total, left_src, right_src, left_mid, right_mid, left_out, right_out,
+    weight, picked, window, total, slots, left_src, right_src, left_mid, right_mid, left_out, right_out,
     arranged, query, keys, mixed, cell_src, cell_mid, cell_turn, weight_sems, late_sems, sems, cell_sems,
 ):
     curve, tile = place_of()
@@ -197,6 +195,8 @@
     )
     up.start()
     down.start()
+    wanted = jnp.concatenate([slot_ref[:, b * BLOCK : (b + 1) * BLOCK] for b in (1, 2, 0, 3)], axis=1)
+    slots[...] = hot(lax.broadcasted_iota(I32, (OWN, ROWS), 0), wanted)
     conv(0, True)
     up.wait()
     down.wait()
@@ -214,11 +214,9 @@
     conv(2 * BLOCK, False)
     own = jnp.concatenate([points_ref[pl.ds(b * BLOCK, BLOCK), :] for b in (1, 2, 0, 3)], axis=0)
     lifted = (own.astype(F32) + gain_ref[...] * norm_rows(total[...])).astype(BF16)
-    wanted = jnp.concatenate([slot_ref[:, b * BLOCK : (b + 1) * BLOCK] for b in (1, 2, 0, 3)], axis=1)
-    slots = hot(lax.broadcasted_iota(I32, (OWN, ROWS), 0), wanted)
 
     def outgoing(first):
-        moved = dot(slots, lifted[:, first : first + C // 2]).reshape(OWNERS, 8, C // 2)
+        moved = dot(slots[...], lifted[:, first : first + C // 2]).reshape(OWNERS, 8, C // 2)
         blocks = jnp.concatenate([moved[:, :, :LANES], moved[:, :, LANES:]], axis=1).astype(BF16)
         return blocks.reshape(CURVE, TILE, 16, LANES)
 
@@ -250,6 +248,11 @@
     tables = jnp.concatenate([from_ref[...], pick_ref[...], jnp.zeros((7, LANES), I32)], axis=0).T
     from_col = jnp.concatenate([tables[:, j : j + 1] for j in range(8)], axis=0)
     pick_col = tables[:, 8:9]
+    copies[0].wait()
+    twice = [room(17 * C, C), room(18 * C, C)]
+    for j in range(2):
+        parts = [wq[:, pl.ds(j * C // 2 + i * SUB, SUB)] for i in range(C // 2 // SUB)]
+        twice[j][...] = jnp.concatenate([x for part in parts for x in (part, part)], axis=1)
     source = lax.broadcasted_iota(I32, (2 * BLOCK, OWN), 1)
     for j in range(4):
         picked[:, pl.ds(j * OWN, OWN)] = hot(from_col[j * 2 * BLOCK : (j + 1) * 2 * BLOCK], source)
@@ -283,9 +286,7 @@
     first = jnp.min(jnp.where(from_ref[...] < OWN, place, OWN), axis=(0, 1), keepdims=True)
     stand_in = dot(hot(lax.broadcasted_iota(I32, (8, OWN), 1), first), normed)[0:1, :]
     normed_keys = jnp.where(live_col, normed.astype(F32), stand_in).astype(BF16)
-    copies[0].wait()
-    halves = [wq[:, pl.ds(j * SUB, SUB)] for j in range(C // SUB)]
-    wide = dot(normed, jnp.concatenate([x for half in halves for x in (half, half)], axis=1)) * SCALE
+    wide = jnp.concatenate([dot(normed, w[...]) for w in twice], axis=1) * SCALE
     copies[1].wait()
     plain = dot(normed_keys, wk[...])
     copies[2].wait()
@@ -341,13 +342,13 @@
     mixed[...] = arranged[...] + dot(attended[...], wo[...])
     for copy in copies[5:]:
         copy.wait()
-    for b in range(OWN // 256):
-        rows = pl.ds(b * 256, 256)
+    for b in range(OWN // 512):
+        rows = pl.ds(b * 512, 512)
         mix = mixed[rows, :]
         second = norm_rows(mix).astype(BF16)
         inner = jnp.concatenate([gelu(dot(second, up[...])).astype(BF16) for up in ups], axis=1)
         fine = mix + dot(inner, wd[...])
-        fine_ref[rows, :] = jnp.where(live_col[b * 256 : (b + 1) * 256], fine, 0.0).astype(BF16)
+        fine_ref[rows, :] = jnp.where(live_col[b * 512 : (b + 1) * 512], fine, 0.0).astype(BF16)
 
     slot = lax.broadcasted_iota(I32, (WIN, OWN), 1) // 8
     cell = lax.broadcasted_iota(I32, (WIN, OWN), 0)
@@ -398,6 +399,7 @@
             pltpu.VMEM((2 * BLOCK, KERNEL * C), BF16),
             pltpu.VMEM((ROWS + 2 * RIM, C), BF16),
             pltpu.VMEM((ROWS, C), F32),
+            pltpu.VMEM((OWN, ROWS), BF16),
         ]
         + [pltpu.VMEM(half, BF16)] * 6
         + [
@@ -418,17 +420,24 @@
     )(*args)
 
 
-def coarse_kernel(fine_ref, land_ref, cell_ref, gain_ref, fine_out, pooled_ref, sem):
-    copy = pltpu.make_async_copy(fine_ref, fine_out, sem)
-    copy.start()
+def coarse_kernel(fine_ref, land_ref, cell_ref, gain_ref, fine_out, pooled_ref, held, sem):
+    pieces = [pl.ds(i * OWN // PIECES, OWN // PIECES) for i in range(PIECES)]
+    into = [pltpu.make_async_copy(fine_ref.at[p], held.at[p], sem.at[0, i]) for i, p in enumerate(pieces)]
+    out = [pltpu.make_async_copy(held.at[p], fine_out.at[p], sem.at[1, i]) for i, p in enumerate(pieces)]
+    for copy in into:
+        copy.start()
     cell_col = jnp.concatenate([cell_ref[...], jnp.zeros((7, LANES), I32)], axis=0).T[:, 0:1]
     cells = lax.broadcasted_iota(I32, (WIN, WIN), 1)
+    for i in range(PIECES):
+        into[i].wait()
+        out[i].start()
     landed = land_ref[...].astype(F32)
     landed = jnp.concatenate([landed[:, :CURVE], landed[:, CURVE:]], axis=2).astype(BF16).reshape(WIN, C)
     source = lax.rem(cells, CURVE) * TILE + lax.div(cells, CURVE)
     gathered = dot(hot(cell_col, source), landed)
     pooled_ref[...] = gelu(gain_ref[...] * norm_rows(gathered)).astype(BF16)
-    copy.wait()
+    for copy in out:
+        copy.wait()
 
 
 def coarse_call(fine, land, cell_from, gain):
@@ -437,9 +446,9 @@
     return pl.pallas_call(
         coarse_kernel,
         out_shape=(jax.ShapeDtypeStruct((OWN, C), BF16), jax.ShapeDtypeStruct((WIN, C), BF16)),
-        in_specs=[vmem] * 4,
+        in_specs=[hbm, vmem, vmem, vmem],
         out_specs=(hbm, vmem),
-        scratch_shapes=[pltpu.SemaphoreType.DMA(())],
+        scratch_shapes=[pltpu.VMEM((OWN, C), BF16), pltpu.SemaphoreType.DMA((2, PIECES))],
     )(fine, land, cell_from, gain)
 
 

time: 102 us -> 102 us (level)
  no operation moved by 1% of the time
where the time goes in v6:
time: 102 us
  Pallas kernels  101 us (99%)
    pallas_call x1, Pallas kernels, block_call(): pl.pallas_call(block_kernel, out_shape=(jax.ShapeDtypeStruct((OWN, C), BF...  97.7 us
    pallas_call x1, Pallas kernels, coarse_call(): pl.pallas_call(coarse_kernel, out_shape=(jax.ShapeDtypeStruct((OWN, C), B...  3.56 us

profile of v6, /device:TPU:1, one launch (start us, length us, event | category | flops | bytes accessed | tf_op | source)
XLA Modules:
  0.0 102.1 jit_solution(10364349831123769521)
XLA Ops:
  0.6 97.7 %shard_map.167 = (bf16[1024,512]{1,0:T(8,128)(2,1)}, bf16[16,16,256]{2,1,0:T(8,128)(2,1)}) custom-call(bf16[512,512]{1,0:T(8,128)(2,1)} %points_ref.1, s32[27,512]{1,0:T(8,128)} %near_ref.1, s32[1,512]{1,0:T(1,128)} %bitcast.8, f32[1,512]{1,0:T(1,128)} %bitcast.9, s32[8,128]{1,0:T(8,128)} %bitcast.7, s32[1,128]{1,0:T(1,128)} %pick_ref.1, ...), custom_call_target="tpu_custom_call" | custom-call | flops 49999998976 | bytes 25000000 | tf_op jit(solution)/shard_map/pallas_call | solution.py:392
  98.4 3.6 %shard_map.168 = (bf16[1024,512]{1,0:T(8,128)(2,1)}, bf16[128,512]{1,0:T(8,128)(2,1)}) custom-call(bf16[1024,512]{1,0:T(8,128)(2,1)} %get-tuple-element.4.fine_ref, bf16[16,16,256]{2,1,0:T(8,128)(2,1)} %get-tuple-element.5.land_ref, s32[1,128]{1,0:T(1,128)} %cell_ref.1, f32[1,512]{1,0:T(1,128)} %bitcast.5), custom_call_target="tpu_custom_call" | custom-call | tf_op jit(solution)/shard_map/pallas_call | solution.py:446

commit v7 on v6

--- a/solution.py
+++ b/solution.py
@@ -35,7 +35,6 @@
 GROUPS = C // LANES
 PER_GROUP = LANES // HEAD
 Q_BLOCK = 512
-PIECES = 4
 SCALE = math.log2(math.e) / math.sqrt(HEAD)
 
 VMEM_LIMIT = 62 * 1024 * 1024
@@ -104,31 +103,6 @@
     def own(self, sem):
         src, dst, _, _, curve, _ = self.args
         return pltpu.make_async_copy(src.at[curve], dst.at[curve], sem)
-
-
-class AlongTile:
-    def __init__(self, src, dst, sems, i, curve, tile):
-        self.args = src, dst, sems, i, curve, tile
-
-    def start(self):
-        src, dst, sems, i, curve, tile = self.args
-
-        @pl.loop(1, TILE)
-        def _(s):
-            peer = lax.rem(tile + s, TILE)
-            send(src.at[:, peer], dst.at[:, tile], sems, i, (curve, peer))
-
-    def wait_recv(self):
-        _, dst, sems, i, _, _ = self.args
-        drain(dst.at[:, pl.ds(0, TILE - 1)], sems.at[i + 1])
-
-    def wait_send(self):
-        src, _, sems, i, _, _ = self.args
-        drain(src.at[:, pl.ds(0, TILE - 1)], sems.at[i])
-
-    def own(self, sem):
-        src, dst, _, _, _, tile = self.args
-        return pltpu.make_async_copy(src.at[:, tile], dst.at[:, tile], sem)
 
 
 def gelu(v):
@@ -196,7 +170,10 @@
     up.start()
     down.start()
     wanted = jnp.concatenate([slot_ref[:, b * BLOCK : (b + 1) * BLOCK] for b in (1, 2, 0, 3)], axis=1)
-    slots[...] = hot(lax.broadcasted_iota(I32, (OWN, ROWS), 0), wanted)
+    inner, outer = wanted & (LANES - 1), wanted & (OWN - LANES)
+    slot = lax.broadcasted_iota(I32, (OWN, ROWS), 0)
+    slots[0] = hot(slot, outer + ((inner + (TILE - tile) * 8) & (LANES - 1)))
+    slots[1] = hot(slot, inner + ((outer + (CURVE - curve) * LANES) & (OWN - LANES)))
     conv(0, True)
     up.wait()
     down.wait()
@@ -215,22 +192,34 @@
     own = jnp.concatenate([points_ref[pl.ds(b * BLOCK, BLOCK), :] for b in (1, 2, 0, 3)], axis=0)
     lifted = (own.astype(F32) + gain_ref[...] * norm_rows(total[...])).astype(BF16)
 
-    def outgoing(first):
-        moved = dot(slots[...], lifted[:, first : first + C // 2]).reshape(OWNERS, 8, C // 2)
+    def outgoing(side):
+        moved = dot(slots[side], lifted[:, side * C // 2 : (side + 1) * C // 2]).reshape(OWNERS, 8, C // 2)
         blocks = jnp.concatenate([moved[:, :, :LANES], moved[:, :, LANES:]], axis=1).astype(BF16)
         return blocks.reshape(CURVE, TILE, 16, LANES)
 
-    left_one = AlongCurve(left_src, left_mid, sems, 0, curve, tile)
-    right_one = AlongTile(right_src, right_mid, sems, 2, curve, tile)
-    left_two = AlongTile(left_mid, left_out, sems, 4, curve, tile)
-    right_two = AlongCurve(right_mid, right_out, sems, 6, curve, tile)
+    half_t, half_c = TILE // 2, CURVE // 2
+    left_sems, right_sems = (0, 14), (2, 16)
     left_src[...] = outgoing(0)
-    left_one.start()
-    left_own = left_one.own(sems.at[8])
+    for q in range(2):
+        part = pl.ds(q * half_t, half_t)
+
+        @pl.loop(1, CURVE)
+        def _(s):
+            peer = lax.rem(curve + s, CURVE)
+            send(left_src.at[peer, part], left_mid.at[curve, part], sems, left_sems[q], (peer, tile))
+
+    left_own = pltpu.make_async_copy(left_src.at[curve], left_mid.at[curve], sems.at[8])
     left_own.start()
-    right_src[...] = outgoing(C // 2)
-    right_one.start()
-    right_own = right_one.own(sems.at[9])
+    right_src[...] = outgoing(1)
+    for q in range(2):
+        part = pl.ds(q * half_c, half_c)
+
+        @pl.loop(1, TILE)
+        def _(s):
+            peer = lax.rem(tile + s, TILE)
+            send(right_src.at[part, peer], right_mid.at[part, tile], sems, right_sems[q], (curve, peer))
+
+    right_own = pltpu.make_async_copy(right_src.at[:, tile], right_mid.at[:, tile], sems.at[9])
     right_own.start()
 
     def room(first, count):
@@ -257,23 +246,35 @@
     for j in range(4):
         picked[:, pl.ds(j * OWN, OWN)] = hot(from_col[j * 2 * BLOCK : (j + 1) * 2 * BLOCK], source)
     left_own.wait()
-    left_one.wait_recv()
-    left_two.start()
-    left_last = left_two.own(sems.at[8])
-    left_last.start()
     right_own.wait()
-    right_one.wait_recv()
-    right_two.start()
-    right_last = right_two.own(sems.at[9])
-    right_last.start()
+    left_last = pltpu.make_async_copy(left_mid.at[:, 0], left_out.at[:, tile], sems.at[8])
+    right_last = pltpu.make_async_copy(right_mid.at[0], right_out.at[curve], sems.at[9])
+    for q in range(2):
+        drain(left_mid.at[pl.ds(0, CURVE - 1), pl.ds(0, half_t)], sems.at[left_sems[q] + 1])
+
+        @pl.loop(max(q * half_t, 1), (q + 1) * half_t)
+        def _(s):
+            send(left_mid.at[:, s], left_out.at[:, tile], sems, 4, (curve, lax.rem(tile + s, TILE)))
+
+        if q == 0:
+            left_last.start()
+        drain(right_mid.at[pl.ds(0, half_c), pl.ds(0, TILE - 1)], sems.at[right_sems[q] + 1])
+
+        @pl.loop(max(q * half_c, 1), (q + 1) * half_c)
+        def _(s):
+            send(right_mid.at[s], right_out.at[curve], sems, 6, (lax.rem(curve + s, CURVE), tile))
+
+        if q == 0:
+            right_last.start()
     left_last.wait()
     right_last.wait()
-    left_two.wait_recv()
-    right_two.wait_recv()
-    left_one.wait_send()
-    right_one.wait_send()
-    left_two.wait_send()
-    right_two.wait_send()
+    drain(left_out.at[:, pl.ds(0, TILE - 1)], sems.at[5])
+    drain(right_out.at[pl.ds(0, CURVE - 1)], sems.at[7])
+    for q in range(2):
+        drain(left_src.at[pl.ds(0, CURVE - 1), pl.ds(0, half_t)], sems.at[left_sems[q]])
+        drain(right_src.at[pl.ds(0, half_c), pl.ds(0, TILE - 1)], sems.at[right_sems[q]])
+    drain(left_mid.at[:, pl.ds(0, TILE - 1)], sems.at[4])
+    drain(right_mid.at[pl.ds(0, CURVE - 1)], sems.at[6])
     left = left_out[...].reshape(OWNERS, 16, LANES).astype(F32)
     right = right_out[...].reshape(OWNERS, 16, LANES).astype(F32)
     got = jnp.concatenate([left[:, :8], left[:, 8:], right[:, :8], right[:, 8:]], axis=2)
@@ -399,7 +400,7 @@
             pltpu.VMEM((2 * BLOCK, KERNEL * C), BF16),
             pltpu.VMEM((ROWS + 2 * RIM, C), BF16),
             pltpu.VMEM((ROWS, C), F32),
-            pltpu.VMEM((OWN, ROWS), BF16),
+            pltpu.VMEM((2, OWN, ROWS), BF16),
         ]
         + [pltpu.VMEM(half, BF16)] * 6
         + [
@@ -412,7 +413,7 @@
             pltpu.VMEM((TILE, 16, C // 2), BF16),
             pltpu.SemaphoreType.DMA((CHUNKS,)),
             pltpu.SemaphoreType.DMA((10,)),
-            pltpu.SemaphoreType.DMA((14,)),
+            pltpu.SemaphoreType.DMA((18,)),
             pltpu.SemaphoreType.DMA((5,)),
         ],
         compiler_params=pltpu.CompilerParams(vmem_limit_bytes=VMEM_LIMIT, collective_id=0, has_side_effects=True),
@@ -420,24 +421,17 @@
     )(*args)
 
 
-def coarse_kernel(fine_ref, land_ref, cell_ref, gain_ref, fine_out, pooled_ref, held, sem):
-    pieces = [pl.ds(i * OWN // PIECES, OWN // PIECES) for i in range(PIECES)]
-    into = [pltpu.make_async_copy(fine_ref.at[p], held.at[p], sem.at[0, i]) for i, p in enumerate(pieces)]
-    out = [pltpu.make_async_copy(held.at[p], fine_out.at[p], sem.at[1, i]) for i, p in enumerate(pieces)]
-    for copy in into:
-        copy.start()
+def coarse_kernel(fine_ref, land_ref, cell_ref, gain_ref, fine_out, pooled_ref, sem):
+    copy = pltpu.make_async_copy(fine_ref, fine_out, sem)
+    copy.start()
     cell_col = jnp.concatenate([cell_ref[...], jnp.zeros((7, LANES), I32)], axis=0).T[:, 0:1]
     cells = lax.broadcasted_iota(I32, (WIN, WIN), 1)
-    for i in range(PIECES):
-        into[i].wait()
-        out[i].start()
     landed = land_ref[...].astype(F32)
     landed = jnp.concatenate([landed[:, :CURVE], landed[:, CURVE:]], axis=2).astype(BF16).reshape(WIN, C)
     source = lax.rem(cells, CURVE) * TILE + lax.div(cells, CURVE)
     gathered = dot(hot(cell_col, source), landed)
     pooled_ref[...] = gelu(gain_ref[...] * norm_rows(gathered)).astype(BF16)
-    for copy in out:
-        copy.wait()
+    copy.wait()
 
 
 def coarse_call(fine, land, cell_from, gain):
@@ -446,9 +440,9 @@
     return pl.pallas_call(
         coarse_kernel,
         out_shape=(jax.ShapeDtypeStruct((OWN, C), BF16), jax.ShapeDtypeStruct((WIN, C), BF16)),
-        in_specs=[hbm, vmem, vmem, vmem],
+        in_specs=[vmem] * 4,
         out_specs=(hbm, vmem),
-        scratch_shapes=[pltpu.VMEM((OWN, C), BF16), pltpu.SemaphoreType.DMA((2, PIECES))],
+        scratch_shapes=[pltpu.SemaphoreType.DMA(())],
     )(fine, land, cell_from, gain)
 
 

time: 102 us -> 104 us (1.020)
  Pallas kernels: 101 us -> 103 us
    pallas_call x1, Pallas kernels: 97.7 us -> 99.8 us  [block_call(): pl.pallas_call(block_kernel, out_shape=(jax.ShapeDtypeStruct((OWN, C), BF...]
where the time goes in v7:
time: 104 us
  Pallas kernels  103 us (99%)
    pallas_call x1, Pallas kernels, block_call(): pl.pallas_call(block_kernel, out_shape=(jax.ShapeDtypeStruct((OWN, C), BF...  99.8 us
    pallas_call x1, Pallas kernels, coarse_call(): pl.pallas_call(coarse_kernel, out_shape=(jax.ShapeDtypeStruct((OWN, C), B...  2.94 us

profile of v7, /device:TPU:1, one launch (start us, length us, event | category | flops | bytes accessed | tf_op | source)
XLA Modules:
  0.0 103.6 jit_solution(67262485474012741)
XLA Ops:
  0.6 99.8 %shard_map.167 = (bf16[1024,512]{1,0:T(8,128)(2,1)}, bf16[16,16,256]{2,1,0:T(8,128)(2,1)}) custom-call(bf16[512,512]{1,0:T(8,128)(2,1)} %points_ref.1, s32[27,512]{1,0:T(8,128)} %near_ref.1, s32[1,512]{1,0:T(1,128)} %bitcast.8, f32[1,512]{1,0:T(1,128)} %bitcast.9, s32[8,128]{1,0:T(8,128)} %bitcast.7, s32[1,128]{1,0:T(1,128)} %pick_ref.1, ...), custom_call_target="tpu_custom_call" | custom-call | flops 49999998976 | bytes 25000000 | tf_op jit(solution)/shard_map/pallas_call | solution.py:393
  100.4 2.9 %shard_map.168 = (bf16[1024,512]{1,0:T(8,128)(2,1)}, bf16[128,512]{1,0:T(8,128)(2,1)}) custom-call(bf16[1024,512]{1,0:T(8,128)(2,1)} %get-tuple-element.4.fine_ref, bf16[16,16,256]{2,1,0:T(8,128)(2,1)} %get-tuple-element.5.land_ref, s32[1,128]{1,0:T(1,128)} %cell_ref.1, f32[1,512]{1,0:T(1,128)} %bitcast.5), custom_call_target="tpu_custom_call" | custom-call | tf_op jit(solution)/shard_map/pallas_call | solution.py:440

commit v8 on v6

--- a/solution.py
+++ b/solution.py
@@ -35,7 +35,6 @@
 GROUPS = C // LANES
 PER_GROUP = LANES // HEAD
 Q_BLOCK = 512
-PIECES = 4
 SCALE = math.log2(math.e) / math.sqrt(HEAD)
 
 VMEM_LIMIT = 62 * 1024 * 1024
@@ -420,24 +419,17 @@
     )(*args)
 
 
-def coarse_kernel(fine_ref, land_ref, cell_ref, gain_ref, fine_out, pooled_ref, held, sem):
-    pieces = [pl.ds(i * OWN // PIECES, OWN // PIECES) for i in range(PIECES)]
-    into = [pltpu.make_async_copy(fine_ref.at[p], held.at[p], sem.at[0, i]) for i, p in enumerate(pieces)]
-    out = [pltpu.make_async_copy(held.at[p], fine_out.at[p], sem.at[1, i]) for i, p in enumerate(pieces)]
-    for copy in into:
-        copy.start()
+def coarse_kernel(fine_ref, land_ref, cell_ref, gain_ref, fine_out, pooled_ref, sem):
+    copy = pltpu.make_async_copy(fine_ref, fine_out, sem)
+    copy.start()
     cell_col = jnp.concatenate([cell_ref[...], jnp.zeros((7, LANES), I32)], axis=0).T[:, 0:1]
     cells = lax.broadcasted_iota(I32, (WIN, WIN), 1)
-    for i in range(PIECES):
-        into[i].wait()
-        out[i].start()
     landed = land_ref[...].astype(F32)
     landed = jnp.concatenate([landed[:, :CURVE], landed[:, CURVE:]], axis=2).astype(BF16).reshape(WIN, C)
     source = lax.rem(cells, CURVE) * TILE + lax.div(cells, CURVE)
     gathered = dot(hot(cell_col, source), landed)
     pooled_ref[...] = gelu(gain_ref[...] * norm_rows(gathered)).astype(BF16)
-    for copy in out:
-        copy.wait()
+    copy.wait()
 
 
 def coarse_call(fine, land, cell_from, gain):
@@ -446,9 +438,9 @@
     return pl.pallas_call(
         coarse_kernel,
         out_shape=(jax.ShapeDtypeStruct((OWN, C), BF16), jax.ShapeDtypeStruct((WIN, C), BF16)),
-        in_specs=[hbm, vmem, vmem, vmem],
+        in_specs=[vmem] * 4,
         out_specs=(hbm, vmem),
-        scratch_shapes=[pltpu.VMEM((OWN, C), BF16), pltpu.SemaphoreType.DMA((2, PIECES))],
+        scratch_shapes=[pltpu.SemaphoreType.DMA(())],
     )(fine, land, cell_from, gain)
 
 

time: 102 us -> 102 us (level)
  no operation moved by 1% of the time
where the time goes in v8:
time: 102 us; the launch traced here: 101 us
  Pallas kernels  101 us (99%)
    pallas_call x1, Pallas kernels, block_call(): pl.pallas_call(block_kernel, out_shape=(jax.ShapeDtypeStruct((OWN, C), BF...  97.7 us
    pallas_call x1, Pallas kernels, coarse_call(): pl.pallas_call(coarse_kernel, out_shape=(jax.ShapeDtypeStruct((OWN, C), B...  2.94 us

profile of v8, /device:TPU:1, one launch (start us, length us, event | category | flops | bytes accessed | tf_op | source)
XLA Modules:
  0.0 101.5 jit_solution(6401429369448657308)
XLA Ops:
  0.6 97.7 %shard_map.167 = (bf16[1024,512]{1,0:T(8,128)(2,1)}, bf16[16,16,256]{2,1,0:T(8,128)(2,1)}) custom-call(bf16[512,512]{1,0:T(8,128)(2,1)} %points_ref.1, s32[27,512]{1,0:T(8,128)} %near_ref.1, s32[1,512]{1,0:T(1,128)} %bitcast.8, f32[1,512]{1,0:T(1,128)} %bitcast.9, s32[8,128]{1,0:T(8,128)} %bitcast.7, s32[1,128]{1,0:T(1,128)} %pick_ref.1, ...), custom_call_target="tpu_custom_call" | custom-call | flops 49999998976 | bytes 25000000 | tf_op jit(solution)/shard_map/pallas_call | solution.py:391
  98.4 2.9 %shard_map.168 = (bf16[1024,512]{1,0:T(8,128)(2,1)}, bf16[128,512]{1,0:T(8,128)(2,1)}) custom-call(bf16[1024,512]{1,0:T(8,128)(2,1)} %get-tuple-element.4.fine_ref, bf16[16,16,256]{2,1,0:T(8,128)(2,1)} %get-tuple-element.5.land_ref, s32[1,128]{1,0:T(1,128)} %cell_ref.1, f32[1,512]{1,0:T(1,128)} %bitcast.5), custom_call_target="tpu_custom_call" | custom-call | tf_op jit(solution)/shard_map/pallas_call | solution.py:438
